TPU v7x, 512 devices: a whole 4x8x8 slice. The times are simulated.
512 devices in a mesh: views: 32 (over x, z), heads: 16 (over y, core).
Axes of the slice: x: 4, y: 8, z: 8, core: 2. Of those that a mesh axis runs over, the one named last changes fastest.
Arguments:
- queries: bfloat16 [8192, 1024], P('views', 'heads'), may hold values from -12 to 12
- keys: bfloat16 [65536, 1024], P('views', 'heads'), may hold values from -6 to 6
- values: bfloat16 [65536, 1024], P('views', 'heads'), may hold values from -6 to 6
- out_weight: bfloat16 [1024, 1024], replicated, may hold values from -0.1875 to 0.1875
Outputs:
- attended: bfloat16 [8192, 1024], P(('views', 'heads'))
All inputs are finite; a program needn't handle non-finite values.
Results may differ from a plain program's by a relative error of at most 0.01265.
Values may be sent and summed in bfloat16 or wider, within the bound.
No kernel may reach another device: no remote copies, remote signals or barrier semaphores. Data moves between devices by JAX's collectives and lax.ppermute only.
A program may use at most 64 MiB of HBM per device.

v0:
```python
import jax
import jax.numpy as jnp
from jax import lax
from jax.sharding import PartitionSpec as P

HEAD_DIM = 64


def per_device(queries, keys, values, out_weight):
    heads_here = keys.shape[1] // HEAD_DIM
    key_count = keys.shape[0]
    scale = HEAD_DIM ** (-0.5)
    gathered = lax.all_gather(queries, "views", axis=0, tiled=True)
    rows = gathered.shape[0]
    block = 512
    key_heads = keys.reshape(key_count, heads_here, HEAD_DIM)
    value_heads = values.reshape(key_count, heads_here, HEAD_DIM)
    query_blocks = gathered.reshape(rows // block, block, heads_here, HEAD_DIM)

    def attend(query_block):
        scores = (
            jnp.einsum("qhd,khd->hqk", query_block, key_heads, preferred_element_type=jnp.float32)
            * scale
        )
        peak = jnp.max(scores, axis=2)
        weights = jnp.exp(scores - peak[:, :, None])
        total = jnp.sum(weights, axis=2)
        summed = jnp.einsum(
            "hqk,khd->qhd",
            weights.astype(jnp.bfloat16),
            value_heads,
            preferred_element_type=jnp.float32,
        )
        return (summed, peak.T, total.T)

    partial_value, peak, total = lax.map(attend, query_blocks)
    partial_value = partial_value.reshape(rows, heads_here, HEAD_DIM)
    peak = peak.reshape(rows, heads_here)
    total = total.reshape(rows, heads_here)
    top = lax.pmax(peak, "views")
    factor = jnp.exp(peak - top)
    summed, denom = (
        lax.psum_scatter(
            partial_value * factor[:, :, None], "views", scatter_dimension=0, tiled=True
        ),
        lax.psum_scatter(total * factor, "views", scatter_dimension=0, tiled=True),
    )
    own_rows = summed.shape[0]
    heads_out = (
        (summed / denom[:, :, None]).astype(jnp.bfloat16).reshape(own_rows, heads_here * HEAD_DIM)
    )
    whole_heads = lax.all_to_all(heads_out, "heads", split_axis=0, concat_axis=1, tiled=True)
    return jnp.dot(whole_heads, out_weight, preferred_element_type=jnp.float32).astype(jnp.bfloat16)


def solution(mesh):
    return jax.shard_map(
        per_device,
        mesh=mesh,
        in_specs=(P("views", "heads"), P("views", "heads"), P("views", "heads"), P()),
        out_specs=P(("views", "heads"), None),
        check_vma=False,
    )
```

profile of v0, /device:TPU:7, one launch (start us, length us, event | category | flops | bytes accessed | tf_op | source)
XLA Modules:
  0.0 828.2 jit_solution(5164944649668951791)
XLA Ops:
  7.3 80.6 %all-gather.2.cloned.1.call-done = bf16[8192,64]{0,1:T(8,128)(2,1)} async-done(((bf16[256,64]{0,1:T(8,128)(2,1)}), bf16[8192,64]{0,1:T(8,128)(2,1)}) %all-gather.2.cloned.1.call-update) | async-done | bytes 1048592 | tf_op jit(solution)/shard_map/all_gather | solution.py:13
  91.1 117.1 %while.14 = (s32[]{:T(128)}, f32[16,512,1,64]{1,0,3,2:T(8,128)}, f32[16,512,1]{1,2,0:T(1,128)S(1)}, f32[16,512,1]{1,2,0:T(1,128)S(1)}, bf16[16,512,1,64]{1,3,2,0...) while((s32[]{:T(128)}, f32[16,512,1,64]{1,0,3,2:T(8,128)}, ...), condition=%wide.region_3.4_spmd, body=%wide.region_0.3_spmd.sunk | while | flops 276823040 | bytes 13845093 | solution.py:36
  94.6 3.8 dynamic_update_slice.16
  102.0 3.8 dynamic_update_slice.16
  109.3 3.8 dynamic_update_slice.16
  116.6 3.8 dynamic_update_slice.16
  123.9 3.8 dynamic_update_slice.16
  131.2 3.8 dynamic_update_slice.16
  138.5 3.8 dynamic_update_slice.16
  145.9 3.8 dynamic_update_slice.16
  153.2 3.8 dynamic_update_slice.16
  160.5 3.8 dynamic_update_slice.16
  167.8 3.8 dynamic_update_slice.16
  175.1 3.8 dynamic_update_slice.16
  182.4 3.8 dynamic_update_slice.16
  189.8 3.8 dynamic_update_slice.16
  197.1 3.8 dynamic_update_slice.16
  204.4 3.8 dynamic_update_slice.16
  208.2 101.1 %pmax.7 = f32[8192,1]{0,1:T(1,128)S(1)} all-reduce(f32[8192,1]{0,1:T(1,128)S(1)} %bitcast.64), channel_id=1, replica_groups=mesh['views'=32,'heads'=16] {'views'}, use_global_device_ids=true, to_apply=%region_4.5 | all-reduce | flops 8192 | bytes 65536 | tf_op jit(solution)/shard_map/pmax | solution.py:40
  309.3 2.7 reshape.96
  314.8 3.1 broadcast_multiply_fusion
  317.8 257.6 %reduce-scatter.7.cloned.1.call-done = f32[256,1]{1,0:T(8,128)} async-done(((f32[8192,1]{1,0:T(8,128)}), f32[256,1]{1,0:T(8,128)}) %reduce-scatter.7.cloned.1.call-update) | async-done | bytes 1040
  576.4 223.2 %reduce-scatter.5.cloned.1.call-done = f32[256,1,64]{0,2,1:T(8,128)} async-done(((f32[8192,1,64]{0,2,1:T(8,128)}), f32[256,1,64]{0,2,1:T(8,128)}) %reduce-scatter.5.cloned.1.call-update) | async-done | bytes 65552 | tf_op jit(solution)/shard_map/reduce_scatter | solution.py:43
  800.7 19.7 %all_to_all.19 = bf16[16,2,512]{2,1,0:T(2,128)(2,1)S(1)} all-to-all(bf16[16,2,512]{2,1,0:T(2,128)(2,1)S(1)} %reshape.101), channel_id=1, replica_groups=mesh['views'=32,'heads'=16] {'heads'}, dimensions={0} | all-to-all | bytes 65536 | tf_op jit(solution)/shard_map/all_to_all | solution.py:52
  (107 shorter events, 66.6 us)
Async XLA Ops:
  6.5 814.1 %copy-start = (bf16[1024,1024]{1,0:T(8,128)(2,1)S(1)}, bf16[1024,1024]{1,0:T(8,128)(2,1)}, u32[]{:S(2)}) copy-start(bf16[1024,1024]{1,0:T(8,128)(2,1)} %param.9) | copy-start | bytes 6291460
  6.5 84.5 %copy-start.2 = (bf16[2048,64]{0,1:T(8,128)(2,1)S(1)}, bf16[2048,64]{0,1:T(8,128)(2,1)}, u32[]{:S(2)}) copy-start(bf16[2048,64]{0,1:T(8,128)(2,1)} %param.8) | copy-start | bytes 786436
  6.5 84.5 %copy-start.1 = (bf16[2048,64]{0,1:T(8,128)(2,1)S(1)}, bf16[2048,64]{0,1:T(8,128)(2,1)}, u32[]{:S(2)}) copy-start(bf16[2048,64]{0,1:T(8,128)(2,1)} %param.7) | copy-start | bytes 786436
  6.5 81.4 %all-gather.2.cloned.1.call-start = ((), (), s32[]{:S(2)}) async-start(), calls=%async_computation.3 | async-start | bytes 1081344 | tf_op jit(solution)/shard_map/all_gather | solution.py:13
  7.3 568.2 %reduce-scatter.7.cloned.1.call-start = ((), (), s32[]{:S(2)}) async-start(), calls=%async_computation.5 | async-start | bytes 4325376
  314.7 484.9 %reduce-scatter.5.cloned.1.call-start = ((), (), s32[]{:S(2)}) async-start(), calls=%async_computation.4 | async-start | bytes 2162688 | tf_op jit(solution)/shard_map/reduce_scatter | solution.py:43
Sparse Core Ops, SparseCore 0:
  10.4 77.4 all-gather.1
  314.8 260.5 reduce-scatter.6
  580.5 219.1 reduce-scatter.4
where the time goes:
time: 832 us; the launch traced here: 828 us
  waiting for transfers between devices  562 us (68%)
  blocking collectives  121 us (15%)
  local copies, waits for them, and re-layouts  72.5 us (9%)
  matrix products  42 us (5%)
  other arithmetic  17.2 us (2%)
  between operations  13.2 us (2%)
    unnamed x4, waiting for transfers between devices  258 us
    reduce_scatter x1, waiting for transfers between devices, per_device(): lax.psum_scatter(partial_value * factor[:, :, None], 'views', scatter_dim...  223 us
    pmax x1, blocking collectives, per_device(): top = lax.pmax(peak, 'views')  101 us
    all_gather x1, waiting for transfers between devices, per_device(): gathered = lax.all_gather(queries, 'views', axis=0, tiled=True)  80.6 us
    dynamic_update_slice x48, local copies, waits for them, and re-layouts, per_device(): partial_value, peak, total = lax.map(attend, query_blocks)  62.6 us
    dot_general x16, matrix products, attend(): jnp.einsum('qhd,khd->hqk', query_block, key_heads, preferred_element_type...  26.4 us
    all_to_all x1, blocking collectives, per_device(): lax.all_to_all(heads_out, 'heads', split_axis=0, concat_axis=1, tiled=True)  19.7 us
  transfers between devices with their start and end apart: 3, of which 3 were waited for; matrix products, arithmetic and copies ran while one was open for 0% of the time, Pallas kernels for 0%

commit v1 on v0

v1 whole, which is shorter than its diff:
```python
import functools

import jax
import jax.numpy as jnp
from jax import lax
from jax.experimental import pallas as pl
from jax.experimental.pallas import tpu as pltpu
from jax.sharding import PartitionSpec as P

HEAD_DIM = 64
LOG2E = 1.4426950408889634
X, Z = 4, 8
ONES = 16
PART = 512
WIDE = 128
LIMIT = 2.0**100
VMEM = 48 * 2**20


def _dot(a, b, ca, cb):
    return lax.dot_general(a, b, (((ca,), (cb,)), ((), ())), preferred_element_type=jnp.float32)


def _attend_kernel(chunks, first, last, *refs):
    q_ref, kv_refs = refs[0], refs[1 : 1 + chunks]
    state_ref = None if first else refs[1 + chunks]
    if last:
        out_ref, hold_ref = refs[-2:]
    else:
        out_ref = hold_ref = refs[-1]
    blocks, _, block = q_ref.shape
    rows = blocks * block
    keys = kv_refs[0].shape[1]
    scale = HEAD_DIM ** (-0.5) * LOG2E
    ones = jnp.ones((ONES, PART), jnp.bfloat16)

    def queries():
        return jnp.concatenate([q_ref[b] for b in range(blocks)], axis=1)

    def score(kv_ref, at, q):
        return _dot(kv_ref[0:HEAD_DIM, pl.ds(at, PART)], q, 0, 0) * scale

    def weigh(kv_ref, at, weights):
        v = jnp.concatenate([kv_ref[HEAD_DIM : 2 * HEAD_DIM, pl.ds(at, PART)], ones], axis=0)
        return _dot(v, weights.astype(jnp.bfloat16), 1, 0)

    q = queries()
    total = jnp.zeros((HEAD_DIM + ONES, rows), jnp.float32) if first else state_ref[...]
    peak = None if first else state_ref[72:73, :]
    for kv_ref in kv_refs:
        for at in range(0, keys, PART):
            s = score(kv_ref, at, q)
            if peak is None:
                peak = jnp.max(s, axis=0, keepdims=True)
            total = total + weigh(kv_ref, at, jnp.exp2(s - peak))
    hold_ref[0:72, :] = total[0:72]
    hold_ref[72:80, :] = jnp.broadcast_to(peak, (8, rows))
    in_range = jnp.max(total[64:65]) < LIMIT

    @pl.when(jnp.logical_not(in_range))
    def _():
        q = queries()
        if first:
            hold_ref[0:72, :] = jnp.zeros((72, rows), jnp.float32)
            hold_ref[72:80, :] = jnp.full((8, rows), -1e30, jnp.float32)
        else:
            hold_ref[...] = state_ref[...]
        for kv_ref in kv_refs:

            @pl.loop(0, keys // PART)
            def _(i):
                at = pl.multiple_of(i * PART, PART)
                s = score(kv_ref, at, q)
                old = hold_ref[72:73, :]
                new = jnp.maximum(old, jnp.max(s, axis=0, keepdims=True))
                more = weigh(kv_ref, at, jnp.exp2(s - new))
                hold_ref[0:72, :] = hold_ref[0:72, :] * jnp.exp2(old - new) + more[0:72]
                hold_ref[72:80, :] = jnp.broadcast_to(new, (8, rows))

    if last:
        def head(x):
            return x.astype(jnp.bfloat16).astype(jnp.float32)

        t = hold_ref[64:72, :]
        p = hold_ref[72:80, :]
        t0 = head(t)
        p0 = head(p)
        p1 = head(p - p0)
        p2 = p - p0 - p1
        at = lax.broadcasted_iota(jnp.int32, (8, rows), 0)
        tail = jnp.where(at == 0, t0, 0.0)
        for i, x in ((1, t - t0), (2, p0), (3, p1), (4, p2)):
            tail = jnp.where(at == i, x, tail)
        both = jnp.concatenate(
            [hold_ref[0:HEAD_DIM, :], tail, jnp.zeros((WIDE - HEAD_DIM - 8, rows), jnp.float32)], axis=0
        )
        out_ref[...] = both.T.astype(jnp.bfloat16)


def _attend(q_all, kvs, state, last):
    blocks, _, block = q_all.shape
    rows = blocks * block
    state_type = jax.ShapeDtypeStruct((80, rows), jnp.float32)
    operands = (q_all, *kvs) + (() if state is None else (state,))
    keys = len(kvs) * kvs[0].shape[1]
    return pl.pallas_call(
        functools.partial(_attend_kernel, len(kvs), state is None, last),
        out_shape=jax.ShapeDtypeStruct((rows, WIDE), jnp.bfloat16) if last else state_type,
        in_specs=[pl.BlockSpec(memory_space=pltpu.VMEM)] * len(operands),
        out_specs=pl.BlockSpec(memory_space=pltpu.VMEM),
        scratch_shapes=[pltpu.VMEM((80, rows), jnp.float32)] if last else [],
        compiler_params=pltpu.CompilerParams(vmem_limit_bytes=VMEM),
        cost_estimate=pl.CostEstimate(
            flops=4 * rows * keys * 256, bytes_accessed=2**21, transcendentals=rows * keys
        ),
    )(*operands)


def _finish_kernel(own, heads, got_ref, weight_ref, out_ref):
    n = heads * own
    col = lax.broadcasted_iota(jnp.int32, (WIDE, 2 * WIDE), 0)
    half = lax.broadcasted_iota(jnp.int32, (WIDE, 2 * WIDE), 1) // WIDE
    pick = ((half == 0) & (col >= 64) & (col < 66)) | ((half == 1) & (col >= 66) & (col < 69))
    pick = jnp.where(pick, 1.0, 0.0).astype(jnp.bfloat16)
    parts = [got_ref[z * n : (z + 1) * n, :] for z in range(Z)]
    spread = [_dot(part, pick, 1, 0) for part in parts]
    top = spread[0][:, WIDE:]
    for s in spread[1:]:
        top = jnp.maximum(top, s[:, WIDE:])
    summed = jnp.zeros((n, WIDE), jnp.float32)
    total = jnp.zeros((n, WIDE), jnp.float32)
    for part, s in zip(parts, spread):
        factor = jnp.exp2(s[:, WIDE:] - top)
        summed += factor * part.astype(jnp.float32)
        total += factor * s[:, :WIDE]
    out = summed / total
    lane = lax.broadcasted_iota(jnp.int32, (own, WIDE), 1)
    acc = jnp.zeros(out_ref.shape, jnp.float32)
    per = 4
    for g in range(heads // per):
        pairs = []
        for h in range(g * per, (g + 1) * per, 2):
            even = out[h * own : (h + 1) * own]
            odd = pltpu.roll(out[(h + 1) * own : (h + 2) * own], HEAD_DIM, 1)
            pairs.append(jnp.where(lane < HEAD_DIM, even, odd).astype(jnp.bfloat16))
        w = weight_ref[g * per * HEAD_DIM : (g + 1) * per * HEAD_DIM, :]
        acc += _dot(jnp.concatenate(pairs, axis=1), w, 1, 0)
    out_ref[...] = acc.astype(jnp.bfloat16)


def _finish(got, out_weight, own, heads):
    return pl.pallas_call(
        functools.partial(_finish_kernel, own, heads),
        out_shape=jax.ShapeDtypeStruct((own, out_weight.shape[1]), jnp.bfloat16),
        in_specs=[pl.BlockSpec(memory_space=pltpu.VMEM)] * 2,
        out_specs=pl.BlockSpec(memory_space=pltpu.VMEM),
        compiler_params=pltpu.CompilerParams(vmem_limit_bytes=VMEM),
    )(got, out_weight)


def per_device(heads, queries, keys, values, out_weight):
    z_groups = [[x * Z + z for z in range(Z)] for x in range(X)]
    zh_groups = [[(x * Z + z) * heads + h for z in range(Z) for h in range(heads)] for x in range(X)]

    def from_x(array, step):
        return lax.ppermute(
            array, "views", [(x * Z + z, (x + step) % X * Z + z) for x in range(X) for z in range(Z)]
        )

    copies = jnp.broadcast_to(queries.T[None], (Z, HEAD_DIM, queries.shape[0]))
    q_all = lax.all_to_all(copies, "views", 0, 0, tiled=True, axis_index_groups=z_groups)
    kv = jnp.concatenate([keys.T, values.T], axis=0)
    kv1, kv3, kv2 = from_x(kv, 1), from_x(kv, 3), from_x(kv, 2)
    state = _attend(q_all, (kv,), None, False)
    state = _attend(q_all, (kv1, kv3), state, False)
    rows = _attend(q_all, (kv2,), state, True)

    own = queries.shape[0] // heads
    sent = rows.reshape(Z * heads, own, WIDE)
    got = lax.all_to_all(sent, ("views", "heads"), 0, 0, tiled=True, axis_index_groups=zh_groups)
    return _finish(got.reshape(Z * heads * own, WIDE), out_weight, own, heads)


def solution(mesh):
    assert mesh.shape["views"] == X * Z
    return jax.shard_map(
        functools.partial(per_device, mesh.shape["heads"]),
        mesh=mesh,
        in_specs=(P("views", "heads"), P("views", "heads"), P("views", "heads"), P()),
        out_specs=P(("views", "heads"), None),
        check_vma=False,
    )
```

time: 832 us -> 103 us (0.12)
  waiting for transfers between devices: 562 us -> 4.5 us
  local copies, waits for them, and re-layouts: 72.5 us -> 1.48 us
  blocking collectives: 121 us -> 58.8 us
  matrix products: 42 us -> 0 us
  Pallas kernels: 0 us -> 18.5 us
  starting transfers between devices: 0.08 us -> 18.4 us
  other arithmetic: 17.2 us -> 1.06 us
  between operations: 13.2 us -> 0.06 us
    unnamed x4 -> x0, waiting for transfers between devices: 258 us -> none
    reduce_scatter x1 -> x0, waiting for transfers between devices: 223 us -> none  [per_device(): lax.psum_scatter(partial_value * factor[:, :, None], 'views', scatter_dim...]
    pmax x1 -> x0, blocking collectives: 101 us -> none  [per_device(): top = lax.pmax(peak, 'views')]
    all_gather x1 -> x0, waiting for transfers between devices: 80.6 us -> none  [per_device(): gathered = lax.all_gather(queries, 'views', axis=0, tiled=True)]
    dynamic_update_slice x48 -> x0, local copies, waits for them, and re-layouts: 62.6 us -> none  [per_device(): partial_value, peak, total = lax.map(attend, query_blocks)]
    dot_general x33 -> x0, matrix products: 42 us -> none  [the longest x16 26.4 us: attend(): jnp.einsum('qhd,khd->hqk', query_block, key_heads, preferred_element_type...]
    all_to_all x1, blocking collectives: 19.7 us -> 58.8 us  [per_device(): lax.all_to_all(sent, ('views', 'heads'), 0, 0, tiled=True, axis_index_gro...]
    pallas_call x0 -> x4, Pallas kernels: none -> 18.5 us  [the longest x3 16.9 us: _attend(): pl.pallas_call(functools.partial(_attend_kernel, len(kvs), state is None,...]
  transfers between devices with their start and end apart: 3 -> 4, of which waited for: 3 -> 3; matrix products, arithmetic and copies ran while one was open for 0% -> 1% of each run, Pallas kernels for 0% -> 12%
where the time goes in v1:
time: 103 us
  blocking collectives  58.8 us (57%)
  Pallas kernels  18.5 us (18%)
  starting transfers between devices  18.4 us (18%)
  waiting for transfers between devices  4.5 us (4%)
  local copies, waits for them, and re-layouts  1.48 us (1%)
  other arithmetic  1.06 us (1%)
    all_to_all x1, blocking collectives, per_device(): lax.all_to_all(sent, ('views', 'heads'), 0, 0, tiled=True, axis_index_gro...  58.8 us
    pallas_call x3, Pallas kernels, _attend(): pl.pallas_call(functools.partial(_attend_kernel, len(kvs), state is None,...  16.9 us
    all_to_all x1, starting transfers between devices, per_device(): lax.all_to_all(copies, 'views', 0, 0, tiled=True, axis_index_groups=z_gro...  10 us
    ppermute x3, starting transfers between devices, from_x(): lax.ppermute(array, 'views', [(x * Z + z, (x + step) % X * Z + z) for x i...  8.41 us
    ppermute x3, waiting for transfers between devices, from_x(): lax.ppermute(array, 'views', [(x * Z + z, (x + step) % X * Z + z) for x i...  3.63 us
  transfers between devices with their start and end apart: 4, of which 3 were waited for; matrix products, arithmetic and copies ran while one was open for 1% of the time, Pallas kernels for 12%

profile of v1, /device:TPU:7, one launch (start us, length us, event | category | flops | bytes accessed | tf_op | source)
XLA Modules:
  0.0 102.8 jit_solution(11094150639812278615)
XLA Ops:
  0.0 1.5 %broadcast_in_dim.2 = bf16[8,64,256]{2,1,0:T(8,128)(2,1)} broadcast(bf16[64,256]{1,0:T(8,128)(2,1)} %bitcast.9), dimensions={1,2} | broadcast | bytes 294912 | tf_op jit(solution)/shard_map/broadcast_in_dim | solution.py:170
  1.5 10.0 %all-to-all-start = ((bf16[8,64,256]{2,1,0:T(8,128)(2,1)}), bf16[8,64,256]{2,1,0:T(8,128)(2,1)S(1)}, u32[]{:S(2)}, u32[]{:S(2)}) async-start(bf16[8,64,256]{2,1,0:T(8,128)(2,1)} %broadcast_in_dim.2), calls=%async_computation | async-start | bytes 524288 | tf_op jit(solution)/shard_map/all_to_all | solution.py:171
  11.5 1.1 %pad_maximum_fusion.refs_1_ = bf16[128,2048]{1,0:T(8,128)(2,1)S(1)} fusion(bf16[64,2048]{1,0:T(8,128)(2,1)} %bitcast.7, bf16[64,2048]{1,0:T(8,128)(2,1)} %bitcast.8), kind=kLoop, calls=%fused_computation | loop fusion | flops 1048576 | bytes 1048576 | tf_op jit(solution)/shard_map/concatenate | solution.py:172
  12.6 2.5 %collective-permute-start.2 = (bf16[128,2048]{1,0:T(8,128)(2,1)S(1)}, bf16[128,2048]{1,0:T(8,128)(2,1)S(1)}, u32[]{:S(2)}, u32[]{:S(2)}) collective-permute-start(bf16[128,2048]{1,0:T(8,128)(2,1)S(1)} %pad_maximum_fusion.refs_1_), channel_id=1, source_target_pairs={{0,384},{16,400},{32,416},{48,432},{64,448},{80,464},{96,480},{112... | collective-permute-start | bytes 1572872 | tf_op jit(solution)/shard_map/ppermute | solution.py:166
  15.0 4.0 %collective-permute-start.1 = (bf16[128,2048]{1,0:T(8,128)(2,1)S(1)}, bf16[128,2048]{1,0:T(8,128)(2,1)S(1)}, u32[]{:S(2)}, u32[]{:S(2)}) collective-permute-start(bf16[128,2048]{1,0:T(8,128)(2,1)S(1)} %pad_maximum_fusion.refs_1_), channel_id=1, source_target_pairs={{0,128},{16,144},{32,160},{48,176},{64,192},{80,208},{96,224},{112... | collective-permute-start | bytes 1572872 | tf_op jit(solution)/shard_map/ppermute | solution.py:166
  19.1 1.9 %collective-permute-start = (bf16[128,2048]{1,0:T(8,128)(2,1)S(1)}, bf16[128,2048]{1,0:T(8,128)(2,1)S(1)}, u32[]{:S(2)}, u32[]{:S(2)}) collective-permute-start(bf16[128,2048]{1,0:T(8,128)(2,1)S(1)} %pad_maximum_fusion.refs_1_), channel_id=1, source_target_pairs={{0,256},{16,272},{32,288},{48,304},{64,320},{80,336},{96,352},{112... | collective-permute-start | bytes 1572872 | tf_op jit(solution)/shard_map/ppermute | solution.py:166
  21.0 0.9 all-to-all-done.refs_0_
  21.9 4.6 %shard_map.46.refs_3_ = f32[80,2048]{1,0:T(8,128)S(1)} custom-call(bf16[8,64,256]{2,1,0:T(8,128)(2,1)S(1)} %all-to-all-done.refs_0_, bf16[128,2048]{1,0:T(8,128)(2,1)S(1)} %pad_maximum_fusion.refs_1_), custom_call_target="tpu_custom_call" | custom-call | flops 4294967296 | bytes 2097152 | tf_op jit(solution)/shard_map/pallas_call | solution.py:106
  26.5 2.9 %collective-permute-done.2.refs_2_ = bf16[128,2048]{1,0:T(8,128)(2,1)S(1)} collective-permute-done((bf16[128,2048]{1,0:T(8,128)(2,1)S(1)}, bf16[128,2048]{1,0:T(8,128)(2,1)S(1)}, u32[]{:S(2)}, u32[]{:S(2)}) %collective-permute-start.2) | collective-permute-done | bytes 524320 | tf_op jit(solution)/shard_map/ppermute | solution.py:166
  29.4 0.0 collective-permute-done.1.refs_1_
  29.5 8.0 %shard_map.47.refs_2_ = f32[80,2048]{1,0:T(8,128)S(1)} custom-call(bf16[8,64,256]{2,1,0:T(8,128)(2,1)S(1)} %all-to-all-done.refs_0_, bf16[128,2048]{1,0:T(8,128)(2,1)S(1)} %collective-permute-done.1.refs_1_, bf16[128,2048]{1,0:T(8,128)(2,1)S(1)} %collective-permute-done.2.refs_2_, f32[80,2048]{1,0:T(8,128)S(1)} %shard_map.46.refs_3_), custom_call_target="tpu_custom_call" | custom-call | flops 8589934592 | bytes 2097152 | tf_op jit(solution)/shard_map/pallas_call | solution.py:106
  37.5 0.7 collective-permute-done.refs_1_
  38.1 0.0 copy-start
  38.1 4.3 %shard_map.48 = bf16[2048,128]{1,0:T(8,128)(2,1)S(1)} custom-call(bf16[8,64,256]{2,1,0:T(8,128)(2,1)S(1)} %all-to-all-done.refs_0_, bf16[128,2048]{1,0:T(8,128)(2,1)S(1)} %collective-permute-done.refs_1_, f32[80,2048]{1,0:T(8,128)S(1)} %shard_map.47.refs_2_), custom_call_target="tpu_custom_call" | custom-call | flops 4294967296 | bytes 2097152 | tf_op jit(solution)/shard_map/pallas_call | solution.py:106
  42.4 58.8 %all_to_all.10 = bf16[128,16,128]{2,1,0:T(8,128)(2,1)S(1)} all-to-all(bf16[128,16,128]{2,1,0:T(8,128)(2,1)S(1)} %bitcast.6), channel_id=1, replica_groups={{0,1,2,3,4,5,6,7,8,9,10,11,12,13,14,15,16,17,18,19,20,21,22,23,24,25,26..., dimensions={0} | all-to-all | bytes 1048576 | tf_op jit(solution)/shard_map/all_to_all | solution.py:180
  101.2 0.0 copy-done
  101.2 1.6 %shard_map.49 = bf16[16,1024]{1,0:T(8,128)(2,1)} custom-call(bf16[2048,128]{1,0:T(8,128)(2,1)S(1)} %bitcast.5, bf16[1024,1024]{1,0:T(8,128)(2,1)S(1)} %copy-done), custom_call_target="tpu_custom_call" | custom-call | tf_op jit(solution)/shard_map/pallas_call | solution.py:152
Async XLA Ops:
  1.5 20.4 %all-to-all-start = ((bf16[8,64,256]{2,1,0:T(8,128)(2,1)}), bf16[8,64,256]{2,1,0:T(8,128)(2,1)S(1)}, u32[]{:S(2)}, u32[]{:S(2)}) async-start(bf16[8,64,256]{2,1,0:T(8,128)(2,1)} %broadcast_in_dim.2), calls=%async_computation | async-start | bytes 524288 | tf_op jit(solution)/shard_map/all_to_all | solution.py:171
  12.6 16.9 %collective-permute-start.2 = (bf16[128,2048]{1,0:T(8,128)(2,1)S(1)}, bf16[128,2048]{1,0:T(8,128)(2,1)S(1)}, u32[]{:S(2)}, u32[]{:S(2)}) collective-permute-start(bf16[128,2048]{1,0:T(8,128)(2,1)S(1)} %pad_maximum_fusion.refs_1_), channel_id=1, source_target_pairs={{0,384},{16,400},{32,416},{48,432},{64,448},{80,464},{96,480},{112... | collective-permute-start | bytes 1572872 | tf_op jit(solution)/shard_map/ppermute | solution.py:166
  15.0 14.4 %collective-permute-start.1 = (bf16[128,2048]{1,0:T(8,128)(2,1)S(1)}, bf16[128,2048]{1,0:T(8,128)(2,1)S(1)}, u32[]{:S(2)}, u32[]{:S(2)}) collective-permute-start(bf16[128,2048]{1,0:T(8,128)(2,1)S(1)} %pad_maximum_fusion.refs_1_), channel_id=1, source_target_pairs={{0,128},{16,144},{32,160},{48,176},{64,192},{80,208},{96,224},{112... | collective-permute-start | bytes 1572872 | tf_op jit(solution)/shard_map/ppermute | solution.py:166
  19.1 19.1 %collective-permute-start = (bf16[128,2048]{1,0:T(8,128)(2,1)S(1)}, bf16[128,2048]{1,0:T(8,128)(2,1)S(1)}, u32[]{:S(2)}, u32[]{:S(2)}) collective-permute-start(bf16[128,2048]{1,0:T(8,128)(2,1)S(1)} %pad_maximum_fusion.refs_1_), channel_id=1, source_target_pairs={{0,256},{16,272},{32,288},{48,304},{64,320},{80,336},{96,352},{112... | collective-permute-start | bytes 1572872 | tf_op jit(solution)/shard_map/ppermute | solution.py:166
  38.1 63.1 %copy-start = (bf16[1024,1024]{1,0:T(8,128)(2,1)S(1)}, bf16[1024,1024]{1,0:T(8,128)(2,1)}, u32[]{:S(2)}) copy-start(bf16[1024,1024]{1,0:T(8,128)(2,1)} %weight_ref.1) | copy-start | bytes 6291460

commit v2 on v1

--- a/solution.py
+++ b/solution.py
@@ -19,6 +19,27 @@
 
 def _dot(a, b, ca, cb):
     return lax.dot_general(a, b, (((ca,), (cb,)), ((), ())), preferred_element_type=jnp.float32)
+
+
+def _prepare_kernel(q_ref, k_ref, v_ref, copies_ref, kv_ref):
+    kv_ref[0:HEAD_DIM, :] = k_ref[...]
+    kv_ref[HEAD_DIM : 2 * HEAD_DIM, :] = v_ref[...]
+    q = q_ref[...]
+    for z in range(Z):
+        copies_ref[z] = q
+
+
+def _prepare(q, k, v):
+    return pl.pallas_call(
+        _prepare_kernel,
+        out_shape=[
+            jax.ShapeDtypeStruct((Z, *q.shape), q.dtype),
+            jax.ShapeDtypeStruct((2 * HEAD_DIM, k.shape[1]), k.dtype),
+        ],
+        in_specs=[pl.BlockSpec(memory_space=pltpu.VMEM)] * 3,
+        out_specs=[pl.BlockSpec(memory_space=pltpu.VMEM)] * 2,
+        compiler_params=pltpu.CompilerParams(vmem_limit_bytes=62 * 2**20),
+    )(q, k, v)
 
 
 def _attend_kernel(chunks, first, last, *refs):
@@ -122,7 +143,7 @@
     half = lax.broadcasted_iota(jnp.int32, (WIDE, 2 * WIDE), 1) // WIDE
     pick = ((half == 0) & (col >= 64) & (col < 66)) | ((half == 1) & (col >= 66) & (col < 69))
     pick = jnp.where(pick, 1.0, 0.0).astype(jnp.bfloat16)
-    parts = [got_ref[z * n : (z + 1) * n, :] for z in range(Z)]
+    parts = [got_ref[i * n : (i + 1) * n, :] for i in range(got_ref.shape[0] // n)]
     spread = [_dot(part, pick, 1, 0) for part in parts]
     top = spread[0][:, WIDE:]
     for s in spread[1:]:
@@ -167,13 +188,13 @@
             array, "views", [(x * Z + z, (x + step) % X * Z + z) for x in range(X) for z in range(Z)]
         )
 
-    copies = jnp.broadcast_to(queries.T[None], (Z, HEAD_DIM, queries.shape[0]))
+    copies, kv = _prepare(queries.T, keys.T, values.T)
+    kv2 = from_x(kv, 2)
     q_all = lax.all_to_all(copies, "views", 0, 0, tiled=True, axis_index_groups=z_groups)
-    kv = jnp.concatenate([keys.T, values.T], axis=0)
-    kv1, kv3, kv2 = from_x(kv, 1), from_x(kv, 3), from_x(kv, 2)
-    state = _attend(q_all, (kv,), None, False)
-    state = _attend(q_all, (kv1, kv3), state, False)
-    rows = _attend(q_all, (kv2,), state, True)
+    kv1, kv3 = from_x(kv, 1), from_x(kv, 3)
+    state = _attend(q_all, (kv, kv2), None, False)
+    state = _attend(q_all, (kv1,), state, False)
+    rows = _attend(q_all, (kv3,), state, True)
 
     own = queries.shape[0] // heads
     sent = rows.reshape(Z * heads, own, WIDE)

time: 103 us -> 89.1 us (0.87)
  the two profiles are of different devices: /device:TPU:7 before, /device:TPU:3 now
where the time goes in v2:
time: 89.1 us; the launch traced here: 88.7 us
  blocking collectives  43.6 us (49%)
  Pallas kernels  20.2 us (23%)
  starting transfers between devices  19.1 us (21%)
  waiting for transfers between devices  4.81 us (5%)
  local copies, waits for them, and re-layouts  1.05 us (1%)
    all_to_all x1, blocking collectives, per_device(): lax.all_to_all(sent, ('views', 'heads'), 0, 0, tiled=True, axis_index_gro...  43.6 us
    pallas_call x3, Pallas kernels, _attend(): pl.pallas_call(functools.partial(_attend_kernel, len(kvs), state is None,...  16.6 us
    all_to_all x1, starting transfers between devices, per_device(): lax.all_to_all(copies, 'views', 0, 0, tiled=True, axis_index_groups=z_gro...  10 us
    ppermute x3, starting transfers between devices, from_x(): lax.ppermute(array, 'views', [(x * Z + z, (x + step) % X * Z + z) for x i...  9.01 us
    all_to_all x1, waiting for transfers between devices, per_device(): lax.all_to_all(copies, 'views', 0, 0, tiled=True, axis_index_groups=z_gro...  4.8 us
    pallas_call x1, Pallas kernels, _prepare(): pl.pallas_call(_prepare_kernel, out_shape=[jax.ShapeDtypeStruct((Z, *q.sh...  1.96 us
  transfers between devices with their start and end apart: 4, of which 1 were waited for; matrix products, arithmetic and copies ran while one was open for 0% of the time, Pallas kernels for 14%

profile of v2, /device:TPU:3, one launch (start us, length us, event | category | flops | bytes accessed | tf_op | source)
XLA Modules:
  0.0 88.7 jit_solution(13257669008970318059)
XLA Ops:
  0.0 2.0 %shard_map.46 = (bf16[8,64,256]{2,1,0:T(8,128)(2,1)}, bf16[128,2048]{1,0:T(8,128)(2,1)}) custom-call(bf16[64,256]{1,0:T(8,128)(2,1)} %bitcast.9, bf16[64,2048]{1,0:T(8,128)(2,1)} %bitcast.7, bf16[64,2048]{1,0:T(8,128)(2,1)} %bitcast.8), custom_call_target="tpu_custom_call" | custom-call | tf_op jit(solution)/shard_map/pallas_call | solution.py:33
  2.0 3.7 %collective-permute-start.2 = (bf16[128,2048]{1,0:T(8,128)(2,1)}, bf16[128,2048]{1,0:T(8,128)(2,1)S(1)}, u32[]{:S(2)}, u32[]{:S(2)}) collective-permute-start(bf16[128,2048]{1,0:T(8,128)(2,1)} %get-tuple-element.8.refs_1_), channel_id=1, source_target_pairs={{0,256},{16,272},{32,288},{48,304},{64,320},{80,336},{96,352},{112... | collective-permute-start | bytes 1572872 | tf_op jit(solution)/shard_map/ppermute | solution.py:187
  5.7 10.0 %all-to-all-start = ((bf16[8,64,256]{2,1,0:T(8,128)(2,1)}), bf16[8,64,256]{2,1,0:T(8,128)(2,1)S(1)}, u32[]{:S(2)}, u32[]{:S(2)}) async-start(bf16[8,64,256]{2,1,0:T(8,128)(2,1)} %get-tuple-element.7), calls=%async_computation | async-start | bytes 524288 | tf_op jit(solution)/shard_map/all_to_all | solution.py:193
  15.8 1.9 %collective-permute-start.1 = (bf16[128,2048]{1,0:T(8,128)(2,1)}, bf16[128,2048]{1,0:T(8,128)(2,1)S(1)}, u32[]{:S(2)}, u32[]{:S(2)}) collective-permute-start(bf16[128,2048]{1,0:T(8,128)(2,1)} %get-tuple-element.8.refs_1_), channel_id=1, source_target_pairs={{0,128},{16,144},{32,160},{48,176},{64,192},{80,208},{96,224},{112... | collective-permute-start | bytes 1572872 | tf_op jit(solution)/shard_map/ppermute | solution.py:187
  17.7 3.4 %collective-permute-start = (bf16[128,2048]{1,0:T(8,128)(2,1)}, bf16[128,2048]{1,0:T(8,128)(2,1)S(1)}, u32[]{:S(2)}, u32[]{:S(2)}) collective-permute-start(bf16[128,2048]{1,0:T(8,128)(2,1)} %get-tuple-element.8.refs_1_), channel_id=1, source_target_pairs={{0,384},{16,400},{32,416},{48,432},{64,448},{80,464},{96,480},{112... | collective-permute-start | bytes 1572872 | tf_op jit(solution)/shard_map/ppermute | solution.py:187
  21.0 4.8 %all-to-all-done.refs_0_ = bf16[8,64,256]{2,1,0:T(8,128)(2,1)S(1)} async-done(((bf16[8,64,256]{2,1,0:T(8,128)(2,1)}), bf16[8,64,256]{2,1,0:T(8,128)(2,1)S(1)}, u32[]{:S(2)}, u32[]{:S(2)}) %all-to-all-start) | async-done | bytes 262176 | tf_op jit(solution)/shard_map/all_to_all | solution.py:193
  25.8 0.0 collective-permute-done.2.refs_2_
  25.9 0.0 copy-start.1
  25.9 1.0 %copy-done.1 = bf16[128,2048]{1,0:T(8,128)(2,1)S(1)} copy-done((bf16[128,2048]{1,0:T(8,128)(2,1)S(1)}, bf16[128,2048]{1,0:T(8,128)(2,1)}, u32[]{:S(2)}) %copy-start.1) | copy-done | bytes 524312
  26.9 8.3 %shard_map.47.refs_2_ = f32[80,2048]{1,0:T(8,128)S(1)} custom-call(bf16[8,64,256]{2,1,0:T(8,128)(2,1)S(1)} %all-to-all-done.refs_0_, bf16[128,2048]{1,0:T(8,128)(2,1)S(1)} %copy-done.1, bf16[128,2048]{1,0:T(8,128)(2,1)S(1)} %collective-permute-done.2.refs_2_), custom_call_target="tpu_custom_call" | custom-call | flops 8589934592 | bytes 2097152 | tf_op jit(solution)/shard_map/pallas_call | solution.py:127
  35.2 0.0 collective-permute-done.1.refs_1_
  35.2 4.0 %shard_map.48.refs_2_ = f32[80,2048]{1,0:T(8,128)S(1)} custom-call(bf16[8,64,256]{2,1,0:T(8,128)(2,1)S(1)} %all-to-all-done.refs_0_, bf16[128,2048]{1,0:T(8,128)(2,1)S(1)} %collective-permute-done.1.refs_1_, f32[80,2048]{1,0:T(8,128)S(1)} %shard_map.47.refs_2_), custom_call_target="tpu_custom_call" | custom-call | flops 4294967296 | bytes 2097152 | tf_op jit(solution)/shard_map/pallas_call | solution.py:127
  39.2 0.0 collective-permute-done.refs_1_
  39.3 0.0 copy-start
  39.3 4.3 %shard_map.49 = bf16[2048,128]{1,0:T(8,128)(2,1)S(1)} custom-call(bf16[8,64,256]{2,1,0:T(8,128)(2,1)S(1)} %all-to-all-done.refs_0_, bf16[128,2048]{1,0:T(8,128)(2,1)S(1)} %collective-permute-done.refs_1_, f32[80,2048]{1,0:T(8,128)S(1)} %shard_map.48.refs_2_), custom_call_target="tpu_custom_call" | custom-call | flops 4294967296 | bytes 2097152 | tf_op jit(solution)/shard_map/pallas_call | solution.py:127
  43.6 43.6 %all_to_all.10 = bf16[128,16,128]{2,1,0:T(8,128)(2,1)S(1)} all-to-all(bf16[128,16,128]{2,1,0:T(8,128)(2,1)S(1)} %bitcast.6), channel_id=1, replica_groups={{0,1,2,3,4,5,6,7,8,9,10,11,12,13,14,15,16,17,18,19,20,21,22,23,24,25,26..., dimensions={0} | all-to-all | bytes 1048576 | tf_op jit(solution)/shard_map/all_to_all | solution.py:201
  87.1 0.0 copy-done
  87.1 1.6 %shard_map.50 = bf16[16,1024]{1,0:T(8,128)(2,1)} custom-call(bf16[2048,128]{1,0:T(8,128)(2,1)S(1)} %bitcast.5, bf16[1024,1024]{1,0:T(8,128)(2,1)S(1)} %copy-done), custom_call_target="tpu_custom_call" | custom-call | tf_op jit(solution)/shard_map/pallas_call | solution.py:173
Async XLA Ops:
  2.0 23.9 %collective-permute-start.2 = (bf16[128,2048]{1,0:T(8,128)(2,1)}, bf16[128,2048]{1,0:T(8,128)(2,1)S(1)}, u32[]{:S(2)}, u32[]{:S(2)}) collective-permute-start(bf16[128,2048]{1,0:T(8,128)(2,1)} %get-tuple-element.8.refs_1_), channel_id=1, source_target_pairs={{0,256},{16,272},{32,288},{48,304},{64,320},{80,336},{96,352},{112... | collective-permute-start | bytes 1572872 | tf_op jit(solution)/shard_map/ppermute | solution.py:187
  5.7 20.1 %all-to-all-start = ((bf16[8,64,256]{2,1,0:T(8,128)(2,1)}), bf16[8,64,256]{2,1,0:T(8,128)(2,1)S(1)}, u32[]{:S(2)}, u32[]{:S(2)}) async-start(bf16[8,64,256]{2,1,0:T(8,128)(2,1)} %get-tuple-element.7), calls=%async_computation | async-start | bytes 524288 | tf_op jit(solution)/shard_map/all_to_all | solution.py:193
  15.8 19.4 %collective-permute-start.1 = (bf16[128,2048]{1,0:T(8,128)(2,1)}, bf16[128,2048]{1,0:T(8,128)(2,1)S(1)}, u32[]{:S(2)}, u32[]{:S(2)}) collective-permute-start(bf16[128,2048]{1,0:T(8,128)(2,1)} %get-tuple-element.8.refs_1_), channel_id=1, source_target_pairs={{0,128},{16,144},{32,160},{48,176},{64,192},{80,208},{96,224},{112... | collective-permute-start | bytes 1572872 | tf_op jit(solution)/shard_map/ppermute | solution.py:187
  17.7 21.6 %collective-permute-start = (bf16[128,2048]{1,0:T(8,128)(2,1)}, bf16[128,2048]{1,0:T(8,128)(2,1)S(1)}, u32[]{:S(2)}, u32[]{:S(2)}) collective-permute-start(bf16[128,2048]{1,0:T(8,128)(2,1)} %get-tuple-element.8.refs_1_), channel_id=1, source_target_pairs={{0,384},{16,400},{32,416},{48,432},{64,448},{80,464},{96,480},{112... | collective-permute-start | bytes 1572872 | tf_op jit(solution)/shard_map/ppermute | solution.py:187
  25.9 1.0 %copy-start.1 = (bf16[128,2048]{1,0:T(8,128)(2,1)S(1)}, bf16[128,2048]{1,0:T(8,128)(2,1)}, u32[]{:S(2)}) copy-start(bf16[128,2048]{1,0:T(8,128)(2,1)} %get-tuple-element.8.refs_1_) | copy-start | bytes 1572868
  39.3 47.9 %copy-start = (bf16[1024,1024]{1,0:T(8,128)(2,1)S(1)}, bf16[1024,1024]{1,0:T(8,128)(2,1)}, u32[]{:S(2)}) copy-start(bf16[1024,1024]{1,0:T(8,128)(2,1)} %weight_ref.1) | copy-start | bytes 6291460

commit v3 on v1

--- a/solution.py
+++ b/solution.py
@@ -13,19 +13,41 @@
 ONES = 16
 PART = 512
 WIDE = 128
+OWN = 16
+SENT = 10
 LIMIT = 2.0**100
 VMEM = 48 * 2**20
 
 
 def _dot(a, b, ca, cb):
     return lax.dot_general(a, b, (((ca,), (cb,)), ((), ())), preferred_element_type=jnp.float32)
+
+
+def _copies_kernel(q_ref, copies_ref):
+    n = q_ref.shape[1]
+    row = lax.broadcasted_iota(jnp.int32, (n, n), 0)
+    to = lax.broadcasted_iota(jnp.int32, (n, n), 1)
+    move = row // OWN * 8 + row % 8 + row % OWN // 8 * (n // 2) == to
+    q = _dot(q_ref[...], jnp.where(move, 1.0, 0.0).astype(jnp.bfloat16), 1, 0).astype(jnp.bfloat16)
+    for z in range(copies_ref.shape[0]):
+        copies_ref[z] = q
+
+
+def _copies(q):
+    return pl.pallas_call(
+        _copies_kernel,
+        out_shape=jax.ShapeDtypeStruct((Z, *q.shape), q.dtype),
+        in_specs=[pl.BlockSpec(memory_space=pltpu.VMEM)],
+        out_specs=pl.BlockSpec(memory_space=pltpu.VMEM),
+        compiler_params=pltpu.CompilerParams(vmem_limit_bytes=62 * 2**20),
+    )(q)
 
 
 def _attend_kernel(chunks, first, last, *refs):
     q_ref, kv_refs = refs[0], refs[1 : 1 + chunks]
     state_ref = None if first else refs[1 + chunks]
     if last:
-        out_ref, hold_ref = refs[-2:]
+        out_ref, hold_ref, pack_ref = refs[-3:]
     else:
         out_ref = hold_ref = refs[-1]
     blocks, _, block = q_ref.shape
@@ -35,7 +57,8 @@
     ones = jnp.ones((ONES, PART), jnp.bfloat16)
 
     def queries():
-        return jnp.concatenate([q_ref[b] for b in range(blocks)], axis=1)
+        parts = [q_ref[b, :, u * block // 2 : (u + 1) * block // 2] for u in range(2) for b in range(blocks)]
+        return jnp.concatenate(parts, axis=1)
 
     def score(kv_ref, at, q):
         return _dot(kv_ref[0:HEAD_DIM, pl.ds(at, PART)], q, 0, 0) * scale
@@ -81,20 +104,31 @@
         def head(x):
             return x.astype(jnp.bfloat16).astype(jnp.float32)
 
+        half = rows // 2
+        count = half // 8
+        both = jnp.concatenate([hold_ref[0:HEAD_DIM, :half], hold_ref[0:HEAD_DIM, half:]], axis=0).T
         t = hold_ref[64:72, :]
         p = hold_ref[72:80, :]
         t0 = head(t)
         p0 = head(p)
         p1 = head(p - p0)
-        p2 = p - p0 - p1
-        at = lax.broadcasted_iota(jnp.int32, (8, rows), 0)
-        tail = jnp.where(at == 0, t0, 0.0)
-        for i, x in ((1, t - t0), (2, p0), (3, p1), (4, p2)):
-            tail = jnp.where(at == i, x, tail)
-        both = jnp.concatenate(
-            [hold_ref[0:HEAD_DIM, :], tail, jnp.zeros((WIDE - HEAD_DIM - 8, rows), jnp.float32)], axis=0
-        )
-        out_ref[...] = both.T.astype(jnp.bfloat16)
+        terms = (t0, t - t0, p0, p1, p - p0 - p1)
+        owner = lax.broadcasted_iota(jnp.int32, (8, WIDE), 0)
+        lane = lax.broadcasted_iota(jnp.int32, (8, WIDE), 1)
+        mine = []
+        for c in range(0, count, 8):
+            at = c * 8 // WIDE * WIDE
+            here = lane // 8 == owner + c % (WIDE // 8)
+            cols = [jnp.where(here, x[:, u * half + at : u * half + at + WIDE], 0.0) for x in terms for u in range(2)]
+            mine.append(jnp.concatenate(cols, axis=1).astype(jnp.bfloat16))
+        source = lax.broadcasted_iota(jnp.int32, (10 * WIDE, WIDE), 0)
+        to = lax.broadcasted_iota(jnp.int32, (10 * WIDE, WIDE), 1)
+        move = jnp.where(source // WIDE * 8 + source % 8 == to, 1.0, 0.0).astype(jnp.bfloat16)
+        tail = _dot(jnp.concatenate(mine, axis=0), move, 1, 0)
+        for c in range(count):
+            pack_ref[c * SENT : c * SENT + 8, :] = both[c * 8 : c * 8 + 8]
+            pack_ref[c * SENT + 8 : c * SENT + 10, :] = jnp.broadcast_to(tail[c : c + 1], (2, WIDE))
+        out_ref[...] = pack_ref[...].astype(jnp.bfloat16)
 
 
 def _attend(q_all, kvs, state, last):
@@ -105,10 +139,12 @@
     keys = len(kvs) * kvs[0].shape[1]
     return pl.pallas_call(
         functools.partial(_attend_kernel, len(kvs), state is None, last),
-        out_shape=jax.ShapeDtypeStruct((rows, WIDE), jnp.bfloat16) if last else state_type,
+        out_shape=jax.ShapeDtypeStruct((rows // OWN * SENT, WIDE), jnp.bfloat16) if last else state_type,
         in_specs=[pl.BlockSpec(memory_space=pltpu.VMEM)] * len(operands),
         out_specs=pl.BlockSpec(memory_space=pltpu.VMEM),
-        scratch_shapes=[pltpu.VMEM((80, rows), jnp.float32)] if last else [],
+        scratch_shapes=[pltpu.VMEM((80, rows), jnp.float32), pltpu.VMEM((rows // OWN * SENT, WIDE), jnp.float32)]
+        if last
+        else [],
         compiler_params=pltpu.CompilerParams(vmem_limit_bytes=VMEM),
         cost_estimate=pl.CostEstimate(
             flops=4 * rows * keys * 256, bytes_accessed=2**21, transcendentals=rows * keys
@@ -116,44 +152,54 @@
     )(*operands)
 
 
-def _finish_kernel(own, heads, got_ref, weight_ref, out_ref):
-    n = heads * own
-    col = lax.broadcasted_iota(jnp.int32, (WIDE, 2 * WIDE), 0)
-    half = lax.broadcasted_iota(jnp.int32, (WIDE, 2 * WIDE), 1) // WIDE
-    pick = ((half == 0) & (col >= 64) & (col < 66)) | ((half == 1) & (col >= 66) & (col < 69))
+def _finish_kernel(heads, got_ref, weight_ref, out_ref, pack_ref):
+    senders = got_ref.shape[0] // (heads * SENT)
+    pack_ref[...] = got_ref[...].astype(jnp.float32)
+    lane = lax.broadcasted_iota(jnp.int32, (8, WIDE), 1)
+    sub = lax.broadcasted_iota(jnp.int32, (8, WIDE), 0)
+    mine = (lane % 8 == sub) & (lane < 5 * OWN)
+    term = lax.broadcasted_iota(jnp.int32, (WIDE, 2 * WIDE), 0)
+    to = lax.broadcasted_iota(jnp.int32, (WIDE, 2 * WIDE), 1)
+    pick = ((term // OWN < 2) == (to < WIDE)) & ((term % OWN < 8) == (to % WIDE < HEAD_DIM))
     pick = jnp.where(pick, 1.0, 0.0).astype(jnp.bfloat16)
-    parts = [got_ref[z * n : (z + 1) * n, :] for z in range(Z)]
-    spread = [_dot(part, pick, 1, 0) for part in parts]
+    parts, spread = [], []
+    for s in range(senders):
+        at = [(s * heads + h) * SENT for h in range(heads)]
+        parts.append(jnp.concatenate([pack_ref[i : i + 8, :] for i in at], axis=0))
+        tails = [jnp.where(mine, jnp.broadcast_to(pack_ref[i + 8 : i + 9, :], (8, WIDE)), 0.0) for i in at]
+        spread.append(_dot(jnp.concatenate(tails, axis=0).astype(jnp.bfloat16), pick, 1, 0))
     top = spread[0][:, WIDE:]
     for s in spread[1:]:
         top = jnp.maximum(top, s[:, WIDE:])
-    summed = jnp.zeros((n, WIDE), jnp.float32)
-    total = jnp.zeros((n, WIDE), jnp.float32)
+    summed = jnp.zeros((8 * heads, WIDE), jnp.float32)
+    total = jnp.zeros((8 * heads, WIDE), jnp.float32)
     for part, s in zip(parts, spread):
         factor = jnp.exp2(s[:, WIDE:] - top)
-        summed += factor * part.astype(jnp.float32)
+        summed += factor * part
         total += factor * s[:, :WIDE]
     out = summed / total
-    lane = lax.broadcasted_iota(jnp.int32, (own, WIDE), 1)
     acc = jnp.zeros(out_ref.shape, jnp.float32)
     per = 4
     for g in range(heads // per):
         pairs = []
         for h in range(g * per, (g + 1) * per, 2):
-            even = out[h * own : (h + 1) * own]
-            odd = pltpu.roll(out[(h + 1) * own : (h + 2) * own], HEAD_DIM, 1)
-            pairs.append(jnp.where(lane < HEAD_DIM, even, odd).astype(jnp.bfloat16))
+            even = out[h * 8 : (h + 1) * 8]
+            odd = out[(h + 1) * 8 : (h + 2) * 8]
+            low = jnp.where(lane < HEAD_DIM, even, pltpu.roll(odd, HEAD_DIM, 1))
+            high = jnp.where(lane < HEAD_DIM, pltpu.roll(even, HEAD_DIM, 1), odd)
+            pairs.append(jnp.concatenate([low, high], axis=0).astype(jnp.bfloat16))
         w = weight_ref[g * per * HEAD_DIM : (g + 1) * per * HEAD_DIM, :]
         acc += _dot(jnp.concatenate(pairs, axis=1), w, 1, 0)
     out_ref[...] = acc.astype(jnp.bfloat16)
 
 
-def _finish(got, out_weight, own, heads):
+def _finish(got, out_weight, heads):
     return pl.pallas_call(
-        functools.partial(_finish_kernel, own, heads),
-        out_shape=jax.ShapeDtypeStruct((own, out_weight.shape[1]), jnp.bfloat16),
+        functools.partial(_finish_kernel, heads),
+        out_shape=jax.ShapeDtypeStruct((OWN, out_weight.shape[1]), jnp.bfloat16),
         in_specs=[pl.BlockSpec(memory_space=pltpu.VMEM)] * 2,
         out_specs=pl.BlockSpec(memory_space=pltpu.VMEM),
+        scratch_shapes=[pltpu.VMEM(got.shape, jnp.float32)],
         compiler_params=pltpu.CompilerParams(vmem_limit_bytes=VMEM),
     )(got, out_weight)
 
@@ -167,18 +213,17 @@
             array, "views", [(x * Z + z, (x + step) % X * Z + z) for x in range(X) for z in range(Z)]
         )
 
-    copies = jnp.broadcast_to(queries.T[None], (Z, HEAD_DIM, queries.shape[0]))
-    q_all = lax.all_to_all(copies, "views", 0, 0, tiled=True, axis_index_groups=z_groups)
     kv = jnp.concatenate([keys.T, values.T], axis=0)
-    kv1, kv3, kv2 = from_x(kv, 1), from_x(kv, 3), from_x(kv, 2)
-    state = _attend(q_all, (kv,), None, False)
-    state = _attend(q_all, (kv1, kv3), state, False)
-    rows = _attend(q_all, (kv2,), state, True)
-
-    own = queries.shape[0] // heads
-    sent = rows.reshape(Z * heads, own, WIDE)
+    kv2 = from_x(kv, 2)
+    q_all = lax.all_to_all(_copies(queries.T), "views", 0, 0, tiled=True, axis_index_groups=z_groups)
+    kv1, kv3 = from_x(kv, 1), from_x(kv, 3)
+    state = _attend(q_all, (kv, kv2), None, False)
+    state = _attend(q_all, (kv1,), state, False)
+    rows = _attend(q_all, (kv3,), state, True)
+
+    sent = rows.reshape(Z * heads * SENT // 2, 2, WIDE)
     got = lax.all_to_all(sent, ("views", "heads"), 0, 0, tiled=True, axis_index_groups=zh_groups)
-    return _finish(got.reshape(Z * heads * own, WIDE), out_weight, own, heads)
+    return _finish(got.reshape(Z * heads * SENT, WIDE), out_weight, heads)
 
 
 def solution(mesh):

time: 103 us -> 83.9 us (0.81)
  the two profiles are of different devices: /device:TPU:7 before, /device:TPU:3 now
where the time goes in v3:
time: 83.9 us; the launch traced here: 83.5 us
  blocking collectives  38.6 us (46%)
  Pallas kernels  19.9 us (24%)
  starting transfers between devices  19.1 us (23%)
  waiting for transfers between devices  4.81 us (6%)
  other arithmetic  1.07 us (1%)
    all_to_all x1, blocking collectives, per_device(): lax.all_to_all(sent, ('views', 'heads'), 0, 0, tiled=True, axis_index_gro...  38.6 us
    pallas_call x3, Pallas kernels, _attend(): pl.pallas_call(functools.partial(_attend_kernel, len(kvs), state is None,...  16.8 us
    all_to_all x1, starting transfers between devices, per_device(): lax.all_to_all(_copies(queries.T), 'views', 0, 0, tiled=True, axis_index_...  10 us
    ppermute x3, starting transfers between devices, from_x(): lax.ppermute(array, 'views', [(x * Z + z, (x + step) % X * Z + z) for x i...  9.02 us
    all_to_all x1, waiting for transfers between devices, per_device(): lax.all_to_all(_copies(queries.T), 'views', 0, 0, tiled=True, axis_index_...  4.8 us
  transfers between devices with their start and end apart: 4, of which 1 were waited for; matrix products, arithmetic and copies ran while one was open for 0% of the time, Pallas kernels for 17%

profile of v3, /device:TPU:3, one launch (start us, length us, event | category | flops | bytes accessed | tf_op | source)
XLA Modules:
  0.0 83.5 jit_solution(7094445558465991225)
XLA Ops:
  0.0 1.1 %pad_maximum_fusion.refs_1_ = bf16[128,2048]{1,0:T(8,128)(2,1)S(1)} fusion(bf16[64,2048]{1,0:T(8,128)(2,1)} %bitcast.7, bf16[64,2048]{1,0:T(8,128)(2,1)} %bitcast.8), kind=kLoop, calls=%fused_computation | loop fusion | flops 1048576 | bytes 1048576 | tf_op jit(solution)/shard_map/concatenate | solution.py:216
  1.1 3.8 %collective-permute-start.2 = (bf16[128,2048]{1,0:T(8,128)(2,1)S(1)}, bf16[128,2048]{1,0:T(8,128)(2,1)S(1)}, u32[]{:S(2)}, u32[]{:S(2)}) collective-permute-start(bf16[128,2048]{1,0:T(8,128)(2,1)S(1)} %pad_maximum_fusion.refs_1_), channel_id=1, source_target_pairs={{0,256},{16,272},{32,288},{48,304},{64,320},{80,336},{96,352},{112... | collective-permute-start | bytes 1572872 | tf_op jit(solution)/shard_map/ppermute | solution.py:212
  4.8 1.7 %shard_map.46 = bf16[8,64,256]{2,1,0:T(8,128)(2,1)} custom-call(bf16[64,256]{1,0:T(8,128)(2,1)} %bitcast.9), custom_call_target="tpu_custom_call" | custom-call | tf_op jit(solution)/shard_map/pallas_call | solution.py:37
  6.5 10.0 %all-to-all-start = ((bf16[8,64,256]{2,1,0:T(8,128)(2,1)}), bf16[8,64,256]{2,1,0:T(8,128)(2,1)S(1)}, u32[]{:S(2)}, u32[]{:S(2)}) async-start(bf16[8,64,256]{2,1,0:T(8,128)(2,1)} %shard_map.46), calls=%async_computation | async-start | bytes 524288 | tf_op jit(solution)/shard_map/all_to_all | solution.py:218
  16.5 1.9 %collective-permute-start.1 = (bf16[128,2048]{1,0:T(8,128)(2,1)S(1)}, bf16[128,2048]{1,0:T(8,128)(2,1)S(1)}, u32[]{:S(2)}, u32[]{:S(2)}) collective-permute-start(bf16[128,2048]{1,0:T(8,128)(2,1)S(1)} %pad_maximum_fusion.refs_1_), channel_id=1, source_target_pairs={{0,128},{16,144},{32,160},{48,176},{64,192},{80,208},{96,224},{112... | collective-permute-start | bytes 1572872 | tf_op jit(solution)/shard_map/ppermute | solution.py:212
  18.5 3.4 %collective-permute-start = (bf16[128,2048]{1,0:T(8,128)(2,1)S(1)}, bf16[128,2048]{1,0:T(8,128)(2,1)S(1)}, u32[]{:S(2)}, u32[]{:S(2)}) collective-permute-start(bf16[128,2048]{1,0:T(8,128)(2,1)S(1)} %pad_maximum_fusion.refs_1_), channel_id=1, source_target_pairs={{0,384},{16,400},{32,416},{48,432},{64,448},{80,464},{96,480},{112... | collective-permute-start | bytes 1572872 | tf_op jit(solution)/shard_map/ppermute | solution.py:212
  21.8 4.8 %all-to-all-done.refs_0_ = bf16[8,64,256]{2,1,0:T(8,128)(2,1)S(1)} async-done(((bf16[8,64,256]{2,1,0:T(8,128)(2,1)}), bf16[8,64,256]{2,1,0:T(8,128)(2,1)S(1)}, u32[]{:S(2)}, u32[]{:S(2)}) %all-to-all-start) | async-done | bytes 262176 | tf_op jit(solution)/shard_map/all_to_all | solution.py:218
  26.6 0.0 collective-permute-done.2.refs_2_
  26.6 8.3 %shard_map.47.refs_2_ = f32[80,2048]{1,0:T(8,128)S(1)} custom-call(bf16[8,64,256]{2,1,0:T(8,128)(2,1)S(1)} %all-to-all-done.refs_0_, bf16[128,2048]{1,0:T(8,128)(2,1)S(1)} %pad_maximum_fusion.refs_1_, bf16[128,2048]{1,0:T(8,128)(2,1)S(1)} %collective-permute-done.2.refs_2_), custom_call_target="tpu_custom_call" | custom-call | flops 8589934592 | bytes 2097152 | tf_op jit(solution)/shard_map/pallas_call | solution.py:140
  34.9 0.0 collective-permute-done.1.refs_1_
  34.9 4.0 %shard_map.48.refs_2_ = f32[80,2048]{1,0:T(8,128)S(1)} custom-call(bf16[8,64,256]{2,1,0:T(8,128)(2,1)S(1)} %all-to-all-done.refs_0_, bf16[128,2048]{1,0:T(8,128)(2,1)S(1)} %collective-permute-done.1.refs_1_, f32[80,2048]{1,0:T(8,128)S(1)} %shard_map.47.refs_2_), custom_call_target="tpu_custom_call" | custom-call | flops 4294967296 | bytes 2097152 | tf_op jit(solution)/shard_map/pallas_call | solution.py:140
  39.0 0.0 collective-permute-done.refs_1_
  39.0 0.0 copy-start
  39.0 4.5 %shard_map.49 = bf16[1280,128]{1,0:T(8,128)(2,1)S(1)} custom-call(bf16[8,64,256]{2,1,0:T(8,128)(2,1)S(1)} %all-to-all-done.refs_0_, bf16[128,2048]{1,0:T(8,128)(2,1)S(1)} %collective-permute-done.refs_1_, f32[80,2048]{1,0:T(8,128)S(1)} %shard_map.48.refs_2_), custom_call_target="tpu_custom_call" | custom-call | flops 4294967296 | bytes 2097152 | tf_op jit(solution)/shard_map/pallas_call | solution.py:140
  43.5 38.6 %all_to_all.10 = bf16[640,2,128]{2,1,0:T(2,128)(2,1)S(1)} all-to-all(bf16[640,2,128]{2,1,0:T(2,128)(2,1)S(1)} %bitcast.6), channel_id=1, replica_groups={{0,1,2,3,4,5,6,7,8,9,10,11,12,13,14,15,16,17,18,19,20,21,22,23,24,25,26..., dimensions={0} | all-to-all | bytes 655360 | tf_op jit(solution)/shard_map/all_to_all | solution.py:225
  82.1 0.0 copy-done
  82.1 1.4 %shard_map.50 = bf16[16,1024]{1,0:T(8,128)(2,1)} custom-call(bf16[1280,128]{1,0:T(8,128)(2,1)S(1)} %bitcast.5, bf16[1024,1024]{1,0:T(8,128)(2,1)S(1)} %copy-done), custom_call_target="tpu_custom_call" | custom-call | tf_op jit(solution)/shard_map/pallas_call | solution.py:197
Async XLA Ops:
  1.1 25.5 %collective-permute-start.2 = (bf16[128,2048]{1,0:T(8,128)(2,1)S(1)}, bf16[128,2048]{1,0:T(8,128)(2,1)S(1)}, u32[]{:S(2)}, u32[]{:S(2)}) collective-permute-start(bf16[128,2048]{1,0:T(8,128)(2,1)S(1)} %pad_maximum_fusion.refs_1_), channel_id=1, source_target_pairs={{0,256},{16,272},{32,288},{48,304},{64,320},{80,336},{96,352},{112... | collective-permute-start | bytes 1572872 | tf_op jit(solution)/shard_map/ppermute | solution.py:212
  6.5 20.1 %all-to-all-start = ((bf16[8,64,256]{2,1,0:T(8,128)(2,1)}), bf16[8,64,256]{2,1,0:T(8,128)(2,1)S(1)}, u32[]{:S(2)}, u32[]{:S(2)}) async-start(bf16[8,64,256]{2,1,0:T(8,128)(2,1)} %shard_map.46), calls=%async_computation | async-start | bytes 524288 | tf_op jit(solution)/shard_map/all_to_all | solution.py:218
  16.5 18.4 %collective-permute-start.1 = (bf16[128,2048]{1,0:T(8,128)(2,1)S(1)}, bf16[128,2048]{1,0:T(8,128)(2,1)S(1)}, u32[]{:S(2)}, u32[]{:S(2)}) collective-permute-start(bf16[128,2048]{1,0:T(8,128)(2,1)S(1)} %pad_maximum_fusion.refs_1_), channel_id=1, source_target_pairs={{0,128},{16,144},{32,160},{48,176},{64,192},{80,208},{96,224},{112... | collective-permute-start | bytes 1572872 | tf_op jit(solution)/shard_map/ppermute | solution.py:212
  18.5 20.5 %collective-permute-start = (bf16[128,2048]{1,0:T(8,128)(2,1)S(1)}, bf16[128,2048]{1,0:T(8,128)(2,1)S(1)}, u32[]{:S(2)}, u32[]{:S(2)}) collective-permute-start(bf16[128,2048]{1,0:T(8,128)(2,1)S(1)} %pad_maximum_fusion.refs_1_), channel_id=1, source_target_pairs={{0,384},{16,400},{32,416},{48,432},{64,448},{80,464},{96,480},{112... | collective-permute-start | bytes 1572872 | tf_op jit(solution)/shard_map/ppermute | solution.py:212
  39.0 43.1 %copy-start = (bf16[1024,1024]{1,0:T(8,128)(2,1)S(1)}, bf16[1024,1024]{1,0:T(8,128)(2,1)}, u32[]{:S(2)}) copy-start(bf16[1024,1024]{1,0:T(8,128)(2,1)} %weight_ref.1) | copy-start | bytes 6291460

commit v4 on v3

--- a/solution.py
+++ b/solution.py
@@ -8,10 +8,11 @@
 from jax.sharding import PartitionSpec as P
 
 HEAD_DIM = 64
-LOG2E = 1.4426950408889634
+SCALE = HEAD_DIM ** (-0.5) * 1.4426950408889634
 X, Z = 4, 8
 ONES = 16
 PART = 512
+FEW = 128
 WIDE = 128
 OWN = 16
 SENT = 10
@@ -39,7 +40,7 @@
         out_shape=jax.ShapeDtypeStruct((Z, *q.shape), q.dtype),
         in_specs=[pl.BlockSpec(memory_space=pltpu.VMEM)],
         out_specs=pl.BlockSpec(memory_space=pltpu.VMEM),
-        compiler_params=pltpu.CompilerParams(vmem_limit_bytes=62 * 2**20),
+        compiler_params=pltpu.CompilerParams(vmem_limit_bytes=8 * 2**20),
     )(q)
 
 
@@ -53,29 +54,38 @@
     blocks, _, block = q_ref.shape
     rows = blocks * block
     keys = kv_refs[0].shape[1]
-    scale = HEAD_DIM ** (-0.5) * LOG2E
+    scale = SCALE
     ones = jnp.ones((ONES, PART), jnp.bfloat16)
 
     def queries():
         parts = [q_ref[b, :, u * block // 2 : (u + 1) * block // 2] for u in range(2) for b in range(blocks)]
         return jnp.concatenate(parts, axis=1)
 
+    def shifted(q, peak):
+        at = lax.broadcasted_iota(jnp.int32, (ONES, rows), 0)
+        return jnp.concatenate([q, jnp.where(at == 0, -peak, 0.0).astype(jnp.bfloat16)], axis=0)
+
+    def highest(s):
+        return jnp.max(s, axis=0, keepdims=True).astype(jnp.bfloat16).astype(jnp.float32)
+
     def score(kv_ref, at, q):
-        return _dot(kv_ref[0:HEAD_DIM, pl.ds(at, PART)], q, 0, 0) * scale
+        return _dot(kv_ref[0:HEAD_DIM, pl.ds(at, PART)], q, 0, 0)
+
+    def shifted_score(kv_ref, at, q):
+        return _dot(jnp.concatenate([kv_ref[0:HEAD_DIM, pl.ds(at, PART)], ones], axis=0), q, 0, 0)
 
     def weigh(kv_ref, at, weights):
         v = jnp.concatenate([kv_ref[HEAD_DIM : 2 * HEAD_DIM, pl.ds(at, PART)], ones], axis=0)
         return _dot(v, weights.astype(jnp.bfloat16), 1, 0)
 
+    total = None if first else state_ref[...]
     q = queries()
-    total = jnp.zeros((HEAD_DIM + ONES, rows), jnp.float32) if first else state_ref[...]
-    peak = None if first else state_ref[72:73, :]
+    peak = highest(_dot(kv_refs[0][0:HEAD_DIM, 0:FEW], q, 0, 0)) if first else state_ref[72:73, :]
+    q = shifted(q, peak)
     for kv_ref in kv_refs:
         for at in range(0, keys, PART):
-            s = score(kv_ref, at, q)
-            if peak is None:
-                peak = jnp.max(s, axis=0, keepdims=True)
-            total = total + weigh(kv_ref, at, jnp.exp2(s - peak))
+            more = weigh(kv_ref, at, jnp.exp2(shifted_score(kv_ref, at, q) * scale))
+            total = more if total is None else total + more
     hold_ref[0:72, :] = total[0:72]
     hold_ref[72:80, :] = jnp.broadcast_to(peak, (8, rows))
     in_range = jnp.max(total[64:65]) < LIMIT
@@ -95,9 +105,9 @@
                 at = pl.multiple_of(i * PART, PART)
                 s = score(kv_ref, at, q)
                 old = hold_ref[72:73, :]
-                new = jnp.maximum(old, jnp.max(s, axis=0, keepdims=True))
-                more = weigh(kv_ref, at, jnp.exp2(s - new))
-                hold_ref[0:72, :] = hold_ref[0:72, :] * jnp.exp2(old - new) + more[0:72]
+                new = jnp.maximum(old, highest(s))
+                more = weigh(kv_ref, at, jnp.exp2((s - new) * scale))
+                hold_ref[0:72, :] = hold_ref[0:72, :] * jnp.exp2((old - new) * scale) + more[0:72]
                 hold_ref[72:80, :] = jnp.broadcast_to(new, (8, rows))
 
     if last:
@@ -110,9 +120,7 @@
         t = hold_ref[64:72, :]
         p = hold_ref[72:80, :]
         t0 = head(t)
-        p0 = head(p)
-        p1 = head(p - p0)
-        terms = (t0, t - t0, p0, p1, p - p0 - p1)
+        terms = (t0, t - t0, p)
         owner = lax.broadcasted_iota(jnp.int32, (8, WIDE), 0)
         lane = lax.broadcasted_iota(jnp.int32, (8, WIDE), 1)
         mine = []
@@ -121,8 +129,8 @@
             here = lane // 8 == owner + c % (WIDE // 8)
             cols = [jnp.where(here, x[:, u * half + at : u * half + at + WIDE], 0.0) for x in terms for u in range(2)]
             mine.append(jnp.concatenate(cols, axis=1).astype(jnp.bfloat16))
-        source = lax.broadcasted_iota(jnp.int32, (10 * WIDE, WIDE), 0)
-        to = lax.broadcasted_iota(jnp.int32, (10 * WIDE, WIDE), 1)
+        source = lax.broadcasted_iota(jnp.int32, (6 * WIDE, WIDE), 0)
+        to = lax.broadcasted_iota(jnp.int32, (6 * WIDE, WIDE), 1)
         move = jnp.where(source // WIDE * 8 + source % 8 == to, 1.0, 0.0).astype(jnp.bfloat16)
         tail = _dot(jnp.concatenate(mine, axis=0), move, 1, 0)
         for c in range(count):
@@ -157,7 +165,7 @@
     pack_ref[...] = got_ref[...].astype(jnp.float32)
     lane = lax.broadcasted_iota(jnp.int32, (8, WIDE), 1)
     sub = lax.broadcasted_iota(jnp.int32, (8, WIDE), 0)
-    mine = (lane % 8 == sub) & (lane < 5 * OWN)
+    mine = (lane % 8 == sub) & (lane < 3 * OWN)
     term = lax.broadcasted_iota(jnp.int32, (WIDE, 2 * WIDE), 0)
     to = lax.broadcasted_iota(jnp.int32, (WIDE, 2 * WIDE), 1)
     pick = ((term // OWN < 2) == (to < WIDE)) & ((term % OWN < 8) == (to % WIDE < HEAD_DIM))
@@ -174,7 +182,7 @@
     summed = jnp.zeros((8 * heads, WIDE), jnp.float32)
     total = jnp.zeros((8 * heads, WIDE), jnp.float32)
     for part, s in zip(parts, spread):
-        factor = jnp.exp2(s[:, WIDE:] - top)
+        factor = jnp.exp2((s[:, WIDE:] - top) * SCALE)
         summed += factor * part
         total += factor * s[:, :WIDE]
     out = summed / total

time: 83.9 us -> 81.8 us (0.975)
  the two profiles are of different devices: /device:TPU:3 before, /device:TPU:7 now
where the time goes in v4:
time: 81.8 us; the launch traced here: 81.4 us
  blocking collectives  38.2 us (47%)
  starting transfers between devices  18.7 us (23%)
  Pallas kernels  18.2 us (22%)
  waiting for transfers between devices  4.44 us (5%)
  other arithmetic  1.06 us (1%)
    all_to_all x1, blocking collectives, per_device(): lax.all_to_all(sent, ('views', 'heads'), 0, 0, tiled=True, axis_index_gro...  38.2 us
    pallas_call x3, Pallas kernels, _attend(): pl.pallas_call(functools.partial(_attend_kernel, len(kvs), state is None,...  15.8 us
    all_to_all x1, starting transfers between devices, per_device(): lax.all_to_all(_copies(queries.T), 'views', 0, 0, tiled=True, axis_index_...  10 us
    ppermute x3, starting transfers between devices, from_x(): lax.ppermute(array, 'views', [(x * Z + z, (x + step) % X * Z + z) for x i...  8.67 us
    all_to_all x1, waiting for transfers between devices, per_device(): lax.all_to_all(_copies(queries.T), 'views', 0, 0, tiled=True, axis_index_...  4.44 us
  transfers between devices with their start and end apart: 4, of which 1 were waited for; matrix products, arithmetic and copies ran while one was open for 0% of the time, Pallas kernels for 15%

profile of v4, /device:TPU:7, one launch (start us, length us, event | category | flops | bytes accessed | tf_op | source)
XLA Modules:
  0.0 81.4 jit_solution(14868642755980384227)
XLA Ops:
  0.0 1.1 %pad_maximum_fusion.refs_1_ = bf16[128,2048]{1,0:T(8,128)(2,1)S(1)} fusion(bf16[64,2048]{1,0:T(8,128)(2,1)} %bitcast.8, bf16[64,2048]{1,0:T(8,128)(2,1)} %bitcast.9), kind=kLoop, calls=%fused_computation | loop fusion | flops 1048576 | bytes 1048576 | tf_op jit(solution)/shard_map/concatenate | solution.py:224
  1.1 3.0 %collective-permute-start.2 = (bf16[128,2048]{1,0:T(8,128)(2,1)S(1)}, bf16[128,2048]{1,0:T(8,128)(2,1)S(1)}, u32[]{:S(2)}, u32[]{:S(2)}) collective-permute-start(bf16[128,2048]{1,0:T(8,128)(2,1)S(1)} %pad_maximum_fusion.refs_1_), channel_id=1, source_target_pairs={{0,256},{16,272},{32,288},{48,304},{64,320},{80,336},{96,352},{112... | collective-permute-start | bytes 1572872 | tf_op jit(solution)/shard_map/ppermute | solution.py:220
  4.1 0.0 copy-start.1
  4.1 0.7 copy-done.1
  4.9 0.9 %shard_map.46 = bf16[8,64,256]{2,1,0:T(8,128)(2,1)} custom-call(bf16[64,256]{1,0:T(8,128)(2,1)S(1)} %bitcast.7), custom_call_target="tpu_custom_call" | custom-call | tf_op jit(solution)/shard_map/pallas_call | solution.py:38
  5.8 10.0 %all-to-all-start = ((bf16[8,64,256]{2,1,0:T(8,128)(2,1)}), bf16[8,64,256]{2,1,0:T(8,128)(2,1)S(1)}, u32[]{:S(2)}, u32[]{:S(2)}) async-start(bf16[8,64,256]{2,1,0:T(8,128)(2,1)} %shard_map.46), calls=%async_computation | async-start | bytes 524288 | tf_op jit(solution)/shard_map/all_to_all | solution.py:226
  15.8 3.7 %collective-permute-start.1 = (bf16[128,2048]{1,0:T(8,128)(2,1)S(1)}, bf16[128,2048]{1,0:T(8,128)(2,1)S(1)}, u32[]{:S(2)}, u32[]{:S(2)}) collective-permute-start(bf16[128,2048]{1,0:T(8,128)(2,1)S(1)} %pad_maximum_fusion.refs_1_), channel_id=1, source_target_pairs={{0,128},{16,144},{32,160},{48,176},{64,192},{80,208},{96,224},{112... | collective-permute-start | bytes 1572872 | tf_op jit(solution)/shard_map/ppermute | solution.py:220
  19.5 1.9 %collective-permute-start = (bf16[128,2048]{1,0:T(8,128)(2,1)S(1)}, bf16[128,2048]{1,0:T(8,128)(2,1)S(1)}, u32[]{:S(2)}, u32[]{:S(2)}) collective-permute-start(bf16[128,2048]{1,0:T(8,128)(2,1)S(1)} %pad_maximum_fusion.refs_1_), channel_id=1, source_target_pairs={{0,384},{16,400},{32,416},{48,432},{64,448},{80,464},{96,480},{112... | collective-permute-start | bytes 1572872 | tf_op jit(solution)/shard_map/ppermute | solution.py:220
  21.5 4.4 %all-to-all-done.refs_0_ = bf16[8,64,256]{2,1,0:T(8,128)(2,1)S(1)} async-done(((bf16[8,64,256]{2,1,0:T(8,128)(2,1)}), bf16[8,64,256]{2,1,0:T(8,128)(2,1)S(1)}, u32[]{:S(2)}, u32[]{:S(2)}) %all-to-all-start) | async-done | bytes 262176 | tf_op jit(solution)/shard_map/all_to_all | solution.py:226
  25.9 0.0 collective-permute-done.2.refs_2_
  25.9 7.8 %shard_map.47.refs_2_ = f32[80,2048]{1,0:T(8,128)S(1)} custom-call(bf16[8,64,256]{2,1,0:T(8,128)(2,1)S(1)} %all-to-all-done.refs_0_, bf16[128,2048]{1,0:T(8,128)(2,1)S(1)} %pad_maximum_fusion.refs_1_, bf16[128,2048]{1,0:T(8,128)(2,1)S(1)} %collective-permute-done.2.refs_2_), custom_call_target="tpu_custom_call" | custom-call | flops 8589934592 | bytes 2097152 | tf_op jit(solution)/shard_map/pallas_call | solution.py:148
  33.7 0.0 collective-permute-done.1.refs_1_
  33.7 3.9 %shard_map.48.refs_2_ = f32[80,2048]{1,0:T(8,128)S(1)} custom-call(bf16[8,64,256]{2,1,0:T(8,128)(2,1)S(1)} %all-to-all-done.refs_0_, bf16[128,2048]{1,0:T(8,128)(2,1)S(1)} %collective-permute-done.1.refs_1_, f32[80,2048]{1,0:T(8,128)S(1)} %shard_map.47.refs_2_), custom_call_target="tpu_custom_call" | custom-call | flops 4294967296 | bytes 2097152 | tf_op jit(solution)/shard_map/pallas_call | solution.py:148
  37.6 0.0 collective-permute-done.refs_1_
  37.6 0.0 copy-start
  37.6 4.2 %shard_map.49 = bf16[1280,128]{1,0:T(8,128)(2,1)S(1)} custom-call(bf16[8,64,256]{2,1,0:T(8,128)(2,1)S(1)} %all-to-all-done.refs_0_, bf16[128,2048]{1,0:T(8,128)(2,1)S(1)} %collective-permute-done.refs_1_, f32[80,2048]{1,0:T(8,128)S(1)} %shard_map.48.refs_2_), custom_call_target="tpu_custom_call" | custom-call | flops 4294967296 | bytes 2097152 | tf_op jit(solution)/shard_map/pallas_call | solution.py:148
  41.8 38.2 %all_to_all.10 = bf16[640,2,128]{2,1,0:T(2,128)(2,1)S(1)} all-to-all(bf16[640,2,128]{2,1,0:T(2,128)(2,1)S(1)} %bitcast.6), channel_id=1, replica_groups={{0,1,2,3,4,5,6,7,8,9,10,11,12,13,14,15,16,17,18,19,20,21,22,23,24,25,26..., dimensions={0} | all-to-all | bytes 655360 | tf_op jit(solution)/shard_map/all_to_all | solution.py:233
  80.0 0.0 copy-done
  80.0 1.4 %shard_map.50 = bf16[16,1024]{1,0:T(8,128)(2,1)} custom-call(bf16[1280,128]{1,0:T(8,128)(2,1)S(1)} %bitcast.5, bf16[1024,1024]{1,0:T(8,128)(2,1)S(1)} %copy-done), custom_call_target="tpu_custom_call" | custom-call | tf_op jit(solution)/shard_map/pallas_call | solution.py:205
Async XLA Ops:
  1.1 24.8 %collective-permute-start.2 = (bf16[128,2048]{1,0:T(8,128)(2,1)S(1)}, bf16[128,2048]{1,0:T(8,128)(2,1)S(1)}, u32[]{:S(2)}, u32[]{:S(2)}) collective-permute-start(bf16[128,2048]{1,0:T(8,128)(2,1)S(1)} %pad_maximum_fusion.refs_1_), channel_id=1, source_target_pairs={{0,256},{16,272},{32,288},{48,304},{64,320},{80,336},{96,352},{112... | collective-permute-start | bytes 1572872 | tf_op jit(solution)/shard_map/ppermute | solution.py:220
  4.1 0.8 copy-start.1
  5.8 20.1 %all-to-all-start = ((bf16[8,64,256]{2,1,0:T(8,128)(2,1)}), bf16[8,64,256]{2,1,0:T(8,128)(2,1)S(1)}, u32[]{:S(2)}, u32[]{:S(2)}) async-start(bf16[8,64,256]{2,1,0:T(8,128)(2,1)} %shard_map.46), calls=%async_computation | async-start | bytes 524288 | tf_op jit(solution)/shard_map/all_to_all | solution.py:226
  15.8 17.9 %collective-permute-start.1 = (bf16[128,2048]{1,0:T(8,128)(2,1)S(1)}, bf16[128,2048]{1,0:T(8,128)(2,1)S(1)}, u32[]{:S(2)}, u32[]{:S(2)}) collective-permute-start(bf16[128,2048]{1,0:T(8,128)(2,1)S(1)} %pad_maximum_fusion.refs_1_), channel_id=1, source_target_pairs={{0,128},{16,144},{32,160},{48,176},{64,192},{80,208},{96,224},{112... | collective-permute-start | bytes 1572872 | tf_op jit(solution)/shard_map/ppermute | solution.py:220
  19.5 18.1 %collective-permute-start = (bf16[128,2048]{1,0:T(8,128)(2,1)S(1)}, bf16[128,2048]{1,0:T(8,128)(2,1)S(1)}, u32[]{:S(2)}, u32[]{:S(2)}) collective-permute-start(bf16[128,2048]{1,0:T(8,128)(2,1)S(1)} %pad_maximum_fusion.refs_1_), channel_id=1, source_target_pairs={{0,384},{16,400},{32,416},{48,432},{64,448},{80,464},{96,480},{112... | collective-permute-start | bytes 1572872 | tf_op jit(solution)/shard_map/ppermute | solution.py:220
  37.6 42.4 %copy-start = (bf16[1024,1024]{1,0:T(8,128)(2,1)S(1)}, bf16[1024,1024]{1,0:T(8,128)(2,1)}, u32[]{:S(2)}) copy-start(bf16[1024,1024]{1,0:T(8,128)(2,1)} %weight_ref.1) | copy-start | bytes 6291460

commit v5 on v4

--- a/solution.py
+++ b/solution.py
@@ -216,15 +216,14 @@
     z_groups = [[x * Z + z for z in range(Z)] for x in range(X)]
     zh_groups = [[(x * Z + z) * heads + h for z in range(Z) for h in range(heads)] for x in range(X)]
 
-    def from_x(array, step):
-        return lax.ppermute(
-            array, "views", [(x * Z + z, (x + step) % X * Z + z) for x in range(X) for z in range(Z)]
-        )
+    def swap_x(array, bits):
+        pairs = [(x * Z + z, (x ^ bits) * Z + z) for x in range(X) for z in range(Z)]
+        return lax.ppermute(array, "views", pairs)
 
     kv = jnp.concatenate([keys.T, values.T], axis=0)
-    kv2 = from_x(kv, 2)
+    kv2 = swap_x(kv, 2)
     q_all = lax.all_to_all(_copies(queries.T), "views", 0, 0, tiled=True, axis_index_groups=z_groups)
-    kv1, kv3 = from_x(kv, 1), from_x(kv, 3)
+    kv1, kv3 = swap_x(kv, 1), swap_x(kv, 3)
     state = _attend(q_all, (kv, kv2), None, False)
     state = _attend(q_all, (kv1,), state, False)
     rows = _attend(q_all, (kv3,), state, True)

time: 81.8 us -> 84.9 us (1.038)
  blocking collectives: 38.2 us -> 40.9 us
    all_to_all x1, blocking collectives: 38.2 us -> 40.9 us  [per_device(): lax.all_to_all(sent, ('views', 'heads'), 0, 0, tiled=True, axis_index_gro...]
where the time goes in v5:
time: 84.9 us; the launch traced here: 84.1 us
  blocking collectives  40.9 us (48%)
  starting transfers between devices  19 us (22%)
  Pallas kernels  18.2 us (21%)
  waiting for transfers between devices  4.14 us (5%)
  other arithmetic  1.06 us (1%)
    all_to_all x1, blocking collectives, per_device(): lax.all_to_all(sent, ('views', 'heads'), 0, 0, tiled=True, axis_index_gro...  40.9 us
    pallas_call x3, Pallas kernels, _attend(): pl.pallas_call(functools.partial(_attend_kernel, len(kvs), state is None,...  15.8 us
    all_to_all x1, starting transfers between devices, per_device(): lax.all_to_all(_copies(queries.T), 'views', 0, 0, tiled=True, axis_index_...  10 us
    ppermute x3, starting transfers between devices, swap_x(): return lax.ppermute(array, 'views', pairs)  8.97 us
    all_to_all x1, waiting for transfers between devices, per_device(): lax.all_to_all(_copies(queries.T), 'views', 0, 0, tiled=True, axis_index_...  4.14 us
  transfers between devices with their start and end apart: 4, of which 1 were waited for; matrix products, arithmetic and copies ran while one was open for 0% of the time, Pallas kernels for 15%

profile of v5, /device:TPU:7, one launch (start us, length us, event | category | flops | bytes accessed | tf_op | source)
XLA Modules:
  0.0 84.1 jit_solution(9212629995956921585)
XLA Ops:
  0.0 1.1 %pad_maximum_fusion.refs_1_ = bf16[128,2048]{1,0:T(8,128)(2,1)S(1)} fusion(bf16[64,2048]{1,0:T(8,128)(2,1)} %bitcast.8, bf16[64,2048]{1,0:T(8,128)(2,1)} %bitcast.9), kind=kLoop, calls=%fused_computation | loop fusion | flops 1048576 | bytes 1048576 | tf_op jit(solution)/shard_map/concatenate | solution.py:223
  1.1 3.0 %collective-permute-start.2 = (bf16[128,2048]{1,0:T(8,128)(2,1)S(1)}, bf16[128,2048]{1,0:T(8,128)(2,1)S(1)}, u32[]{:S(2)}, u32[]{:S(2)}) collective-permute-start(bf16[128,2048]{1,0:T(8,128)(2,1)S(1)} %pad_maximum_fusion.refs_1_), channel_id=1, source_target_pairs={{0,256},{16,272},{32,288},{48,304},{64,320},{80,336},{96,352},{112... | collective-permute-start | bytes 1572872 | tf_op jit(solution)/shard_map/ppermute | solution.py:221
  4.1 0.0 copy-start.1
  4.1 0.7 copy-done.1
  4.9 0.9 %shard_map.46 = bf16[8,64,256]{2,1,0:T(8,128)(2,1)} custom-call(bf16[64,256]{1,0:T(8,128)(2,1)S(1)} %bitcast.7), custom_call_target="tpu_custom_call" | custom-call | tf_op jit(solution)/shard_map/pallas_call | solution.py:38
  5.8 10.0 %all-to-all-start = ((bf16[8,64,256]{2,1,0:T(8,128)(2,1)}), bf16[8,64,256]{2,1,0:T(8,128)(2,1)S(1)}, u32[]{:S(2)}, u32[]{:S(2)}) async-start(bf16[8,64,256]{2,1,0:T(8,128)(2,1)} %shard_map.46), calls=%async_computation | async-start | bytes 524288 | tf_op jit(solution)/shard_map/all_to_all | solution.py:225
  15.8 1.9 %collective-permute-start.1 = (bf16[128,2048]{1,0:T(8,128)(2,1)S(1)}, bf16[128,2048]{1,0:T(8,128)(2,1)S(1)}, u32[]{:S(2)}, u32[]{:S(2)}) collective-permute-start(bf16[128,2048]{1,0:T(8,128)(2,1)S(1)} %pad_maximum_fusion.refs_1_), channel_id=1, source_target_pairs={{0,128},{16,144},{32,160},{48,176},{64,192},{80,208},{96,224},{112... | collective-permute-start | bytes 1572872 | tf_op jit(solution)/shard_map/ppermute | solution.py:221
  17.7 4.0 %collective-permute-start = (bf16[128,2048]{1,0:T(8,128)(2,1)S(1)}, bf16[128,2048]{1,0:T(8,128)(2,1)S(1)}, u32[]{:S(2)}, u32[]{:S(2)}) collective-permute-start(bf16[128,2048]{1,0:T(8,128)(2,1)S(1)} %pad_maximum_fusion.refs_1_), channel_id=1, source_target_pairs={{0,384},{16,400},{32,416},{48,432},{64,448},{80,464},{96,480},{112... | collective-permute-start | bytes 1572872 | tf_op jit(solution)/shard_map/ppermute | solution.py:221
  21.8 4.1 %all-to-all-done.refs_0_ = bf16[8,64,256]{2,1,0:T(8,128)(2,1)S(1)} async-done(((bf16[8,64,256]{2,1,0:T(8,128)(2,1)}), bf16[8,64,256]{2,1,0:T(8,128)(2,1)S(1)}, u32[]{:S(2)}, u32[]{:S(2)}) %all-to-all-start) | async-done | bytes 262176 | tf_op jit(solution)/shard_map/all_to_all | solution.py:225
  25.9 0.0 collective-permute-done.2.refs_2_
  25.9 7.8 %shard_map.47.refs_2_ = f32[80,2048]{1,0:T(8,128)S(1)} custom-call(bf16[8,64,256]{2,1,0:T(8,128)(2,1)S(1)} %all-to-all-done.refs_0_, bf16[128,2048]{1,0:T(8,128)(2,1)S(1)} %pad_maximum_fusion.refs_1_, bf16[128,2048]{1,0:T(8,128)(2,1)S(1)} %collective-permute-done.2.refs_2_), custom_call_target="tpu_custom_call" | custom-call | flops 8589934592 | bytes 2097152 | tf_op jit(solution)/shard_map/pallas_call | solution.py:148
  33.7 0.0 collective-permute-done.1.refs_1_
  33.7 3.9 %shard_map.48.refs_2_ = f32[80,2048]{1,0:T(8,128)S(1)} custom-call(bf16[8,64,256]{2,1,0:T(8,128)(2,1)S(1)} %all-to-all-done.refs_0_, bf16[128,2048]{1,0:T(8,128)(2,1)S(1)} %collective-permute-done.1.refs_1_, f32[80,2048]{1,0:T(8,128)S(1)} %shard_map.47.refs_2_), custom_call_target="tpu_custom_call" | custom-call | flops 4294967296 | bytes 2097152 | tf_op jit(solution)/shard_map/pallas_call | solution.py:148
  37.6 0.0 collective-permute-done.refs_1_
  37.6 0.0 copy-start
  37.6 4.2 %shard_map.49 = bf16[1280,128]{1,0:T(8,128)(2,1)S(1)} custom-call(bf16[8,64,256]{2,1,0:T(8,128)(2,1)S(1)} %all-to-all-done.refs_0_, bf16[128,2048]{1,0:T(8,128)(2,1)S(1)} %collective-permute-done.refs_1_, f32[80,2048]{1,0:T(8,128)S(1)} %shard_map.48.refs_2_), custom_call_target="tpu_custom_call" | custom-call | flops 4294967296 | bytes 2097152 | tf_op jit(solution)/shard_map/pallas_call | solution.py:148
  41.8 40.9 %all_to_all.10 = bf16[640,2,128]{2,1,0:T(2,128)(2,1)S(1)} all-to-all(bf16[640,2,128]{2,1,0:T(2,128)(2,1)S(1)} %bitcast.6), channel_id=1, replica_groups={{0,1,2,3,4,5,6,7,8,9,10,11,12,13,14,15,16,17,18,19,20,21,22,23,24,25,26..., dimensions={0} | all-to-all | bytes 655360 | tf_op jit(solution)/shard_map/all_to_all | solution.py:232
  82.7 0.0 copy-done
  82.7 1.4 %shard_map.50 = bf16[16,1024]{1,0:T(8,128)(2,1)} custom-call(bf16[1280,128]{1,0:T(8,128)(2,1)S(1)} %bitcast.5, bf16[1024,1024]{1,0:T(8,128)(2,1)S(1)} %copy-done), custom_call_target="tpu_custom_call" | custom-call | tf_op jit(solution)/shard_map/pallas_call | solution.py:205
Async XLA Ops:
  1.1 24.8 %collective-permute-start.2 = (bf16[128,2048]{1,0:T(8,128)(2,1)S(1)}, bf16[128,2048]{1,0:T(8,128)(2,1)S(1)}, u32[]{:S(2)}, u32[]{:S(2)}) collective-permute-start(bf16[128,2048]{1,0:T(8,128)(2,1)S(1)} %pad_maximum_fusion.refs_1_), channel_id=1, source_target_pairs={{0,256},{16,272},{32,288},{48,304},{64,320},{80,336},{96,352},{112... | collective-permute-start | bytes 1572872 | tf_op jit(solution)/shard_map/ppermute | solution.py:221
  4.1 0.8 copy-start.1
  5.8 20.1 %all-to-all-start = ((bf16[8,64,256]{2,1,0:T(8,128)(2,1)}), bf16[8,64,256]{2,1,0:T(8,128)(2,1)S(1)}, u32[]{:S(2)}, u32[]{:S(2)}) async-start(bf16[8,64,256]{2,1,0:T(8,128)(2,1)} %shard_map.46), calls=%async_computation | async-start | bytes 524288 | tf_op jit(solution)/shard_map/all_to_all | solution.py:225
  15.8 17.9 %collective-permute-start.1 = (bf16[128,2048]{1,0:T(8,128)(2,1)S(1)}, bf16[128,2048]{1,0:T(8,128)(2,1)S(1)}, u32[]{:S(2)}, u32[]{:S(2)}) collective-permute-start(bf16[128,2048]{1,0:T(8,128)(2,1)S(1)} %pad_maximum_fusion.refs_1_), channel_id=1, source_target_pairs={{0,128},{16,144},{32,160},{48,176},{64,192},{80,208},{96,224},{112... | collective-permute-start | bytes 1572872 | tf_op jit(solution)/shard_map/ppermute | solution.py:221
  17.7 19.9 %collective-permute-start = (bf16[128,2048]{1,0:T(8,128)(2,1)S(1)}, bf16[128,2048]{1,0:T(8,128)(2,1)S(1)}, u32[]{:S(2)}, u32[]{:S(2)}) collective-permute-start(bf16[128,2048]{1,0:T(8,128)(2,1)S(1)} %pad_maximum_fusion.refs_1_), channel_id=1, source_target_pairs={{0,384},{16,400},{32,416},{48,432},{64,448},{80,464},{96,480},{112... | collective-permute-start | bytes 1572872 | tf_op jit(solution)/shard_map/ppermute | solution.py:221
  37.6 45.1 %copy-start = (bf16[1024,1024]{1,0:T(8,128)(2,1)S(1)}, bf16[1024,1024]{1,0:T(8,128)(2,1)}, u32[]{:S(2)}) copy-start(bf16[1024,1024]{1,0:T(8,128)(2,1)} %weight_ref.1) | copy-start | bytes 6291460

commit v6 on v5

--- a/solution.py
+++ b/solution.py
@@ -10,9 +10,10 @@
 HEAD_DIM = 64
 SCALE = HEAD_DIM ** (-0.5) * 1.4426950408889634
 X, Z = 4, 8
+ORDER = (0, 2, 4, 6, 7, 5, 3, 1)
 ONES = 16
 PART = 512
-FEW = 128
+FEW = 64
 WIDE = 128
 OWN = 16
 SENT = 10
@@ -213,8 +214,8 @@
 
 
 def per_device(heads, queries, keys, values, out_weight):
-    z_groups = [[x * Z + z for z in range(Z)] for x in range(X)]
-    zh_groups = [[(x * Z + z) * heads + h for z in range(Z) for h in range(heads)] for x in range(X)]
+    z_groups = [[x * Z + z for z in ORDER] for x in range(X)]
+    zh_groups = [[(x * Z + z) * heads + h for z in ORDER for h in range(heads)] for x in range(X)]
 
     def swap_x(array, bits):
         pairs = [(x * Z + z, (x ^ bits) * Z + z) for x in range(X) for z in range(Z)]

time: 84.9 us -> 83.8 us (0.987)
  the two profiles are of different devices: /device:TPU:7 before, /device:TPU:3 now
where the time goes in v6:
time: 83.8 us; the launch traced here: 83.4 us
  blocking collectives  41.3 us (49%)
  starting transfers between devices  19 us (23%)
  Pallas kernels  18.2 us (22%)
  waiting for transfers between devices  3.09 us (4%)
  other arithmetic  1.06 us (1%)
    all_to_all x1, blocking collectives, per_device(): lax.all_to_all(sent, ('views', 'heads'), 0, 0, tiled=True, axis_index_gro...  41.3 us
    pallas_call x3, Pallas kernels, _attend(): pl.pallas_call(functools.partial(_attend_kernel, len(kvs), state is None,...  15.8 us
    all_to_all x1, starting transfers between devices, per_device(): lax.all_to_all(_copies(queries.T), 'views', 0, 0, tiled=True, axis_index_...  10 us
    ppermute x3, starting transfers between devices, swap_x(): return lax.ppermute(array, 'views', pairs)  8.97 us
    all_to_all x1, waiting for transfers between devices, per_device(): lax.all_to_all(_copies(queries.T), 'views', 0, 0, tiled=True, axis_index_...  3.09 us
  transfers between devices with their start and end apart: 4, of which 1 were waited for; matrix products, arithmetic and copies ran while one was open for 0% of the time, Pallas kernels for 15%

profile of v6, /device:TPU:3, one launch (start us, length us, event | category | flops | bytes accessed | tf_op | source)
XLA Modules:
  0.0 83.4 jit_solution(11065655710730613117)
XLA Ops:
  0.0 1.1 %pad_maximum_fusion.refs_1_ = bf16[128,2048]{1,0:T(8,128)(2,1)S(1)} fusion(bf16[64,2048]{1,0:T(8,128)(2,1)} %bitcast.8, bf16[64,2048]{1,0:T(8,128)(2,1)} %bitcast.9), kind=kLoop, calls=%fused_computation | loop fusion | flops 1048576 | bytes 1048576 | tf_op jit(solution)/shard_map/concatenate | solution.py:224
  1.1 3.8 %collective-permute-start.2 = (bf16[128,2048]{1,0:T(8,128)(2,1)S(1)}, bf16[128,2048]{1,0:T(8,128)(2,1)S(1)}, u32[]{:S(2)}, u32[]{:S(2)}) collective-permute-start(bf16[128,2048]{1,0:T(8,128)(2,1)S(1)} %pad_maximum_fusion.refs_1_), channel_id=1, source_target_pairs={{0,256},{16,272},{32,288},{48,304},{64,320},{80,336},{96,352},{112... | collective-permute-start | bytes 1572872 | tf_op jit(solution)/shard_map/ppermute | solution.py:222
  4.8 0.0 copy-start.1
  4.8 0.7 copy-done.1
  5.6 0.9 %shard_map.46 = bf16[8,64,256]{2,1,0:T(8,128)(2,1)} custom-call(bf16[64,256]{1,0:T(8,128)(2,1)S(1)} %bitcast.7), custom_call_target="tpu_custom_call" | custom-call | tf_op jit(solution)/shard_map/pallas_call | solution.py:39
  6.5 10.0 %all-to-all-start = ((bf16[8,64,256]{2,1,0:T(8,128)(2,1)}), bf16[8,64,256]{2,1,0:T(8,128)(2,1)S(1)}, u32[]{:S(2)}, u32[]{:S(2)}) async-start(bf16[8,64,256]{2,1,0:T(8,128)(2,1)} %shard_map.46), calls=%async_computation | async-start | bytes 524288 | tf_op jit(solution)/shard_map/all_to_all | solution.py:226
  16.5 3.0 %collective-permute-start.1 = (bf16[128,2048]{1,0:T(8,128)(2,1)S(1)}, bf16[128,2048]{1,0:T(8,128)(2,1)S(1)}, u32[]{:S(2)}, u32[]{:S(2)}) collective-permute-start(bf16[128,2048]{1,0:T(8,128)(2,1)S(1)} %pad_maximum_fusion.refs_1_), channel_id=1, source_target_pairs={{0,128},{16,144},{32,160},{48,176},{64,192},{80,208},{96,224},{112... | collective-permute-start | bytes 1572872 | tf_op jit(solution)/shard_map/ppermute | solution.py:222
  19.6 2.2 %collective-permute-start = (bf16[128,2048]{1,0:T(8,128)(2,1)S(1)}, bf16[128,2048]{1,0:T(8,128)(2,1)S(1)}, u32[]{:S(2)}, u32[]{:S(2)}) collective-permute-start(bf16[128,2048]{1,0:T(8,128)(2,1)S(1)} %pad_maximum_fusion.refs_1_), channel_id=1, source_target_pairs={{0,384},{16,400},{32,416},{48,432},{64,448},{80,464},{96,480},{112... | collective-permute-start | bytes 1572872 | tf_op jit(solution)/shard_map/ppermute | solution.py:222
  21.8 3.1 %all-to-all-done.refs_0_ = bf16[8,64,256]{2,1,0:T(8,128)(2,1)S(1)} async-done(((bf16[8,64,256]{2,1,0:T(8,128)(2,1)}), bf16[8,64,256]{2,1,0:T(8,128)(2,1)S(1)}, u32[]{:S(2)}, u32[]{:S(2)}) %all-to-all-start) | async-done | bytes 262176 | tf_op jit(solution)/shard_map/all_to_all | solution.py:226
  24.9 0.0 collective-permute-done.2.refs_2_
  24.9 7.8 %shard_map.47.refs_2_ = f32[80,2048]{1,0:T(8,128)S(1)} custom-call(bf16[8,64,256]{2,1,0:T(8,128)(2,1)S(1)} %all-to-all-done.refs_0_, bf16[128,2048]{1,0:T(8,128)(2,1)S(1)} %pad_maximum_fusion.refs_1_, bf16[128,2048]{1,0:T(8,128)(2,1)S(1)} %collective-permute-done.2.refs_2_), custom_call_target="tpu_custom_call" | custom-call | flops 8589934592 | bytes 2097152 | tf_op jit(solution)/shard_map/pallas_call | solution.py:149
  32.6 0.0 collective-permute-done.1.refs_1_
  32.7 3.9 %shard_map.48.refs_2_ = f32[80,2048]{1,0:T(8,128)S(1)} custom-call(bf16[8,64,256]{2,1,0:T(8,128)(2,1)S(1)} %all-to-all-done.refs_0_, bf16[128,2048]{1,0:T(8,128)(2,1)S(1)} %collective-permute-done.1.refs_1_, f32[80,2048]{1,0:T(8,128)S(1)} %shard_map.47.refs_2_), custom_call_target="tpu_custom_call" | custom-call | flops 4294967296 | bytes 2097152 | tf_op jit(solution)/shard_map/pallas_call | solution.py:149
  36.5 0.0 collective-permute-done.refs_1_
  36.5 0.0 copy-start
  36.5 4.2 %shard_map.49 = bf16[1280,128]{1,0:T(8,128)(2,1)S(1)} custom-call(bf16[8,64,256]{2,1,0:T(8,128)(2,1)S(1)} %all-to-all-done.refs_0_, bf16[128,2048]{1,0:T(8,128)(2,1)S(1)} %collective-permute-done.refs_1_, f32[80,2048]{1,0:T(8,128)S(1)} %shard_map.48.refs_2_), custom_call_target="tpu_custom_call" | custom-call | flops 4294967296 | bytes 2097152 | tf_op jit(solution)/shard_map/pallas_call | solution.py:149
  40.7 41.3 %all_to_all.10 = bf16[640,2,128]{2,1,0:T(2,128)(2,1)S(1)} all-to-all(bf16[640,2,128]{2,1,0:T(2,128)(2,1)S(1)} %bitcast.6), channel_id=1, replica_groups={{0,1,2,3,4,5,6,7,8,9,10,11,12,13,14,15,32,33,34,35,36,37,38,39,40,41,42..., dimensions={0} | all-to-all | bytes 655360 | tf_op jit(solution)/shard_map/all_to_all | solution.py:233
  82.0 0.0 copy-done
  82.0 1.4 %shard_map.50 = bf16[16,1024]{1,0:T(8,128)(2,1)} custom-call(bf16[1280,128]{1,0:T(8,128)(2,1)S(1)} %bitcast.5, bf16[1024,1024]{1,0:T(8,128)(2,1)S(1)} %copy-done), custom_call_target="tpu_custom_call" | custom-call | tf_op jit(solution)/shard_map/pallas_call | solution.py:206
Async XLA Ops:
  1.1 23.8 %collective-permute-start.2 = (bf16[128,2048]{1,0:T(8,128)(2,1)S(1)}, bf16[128,2048]{1,0:T(8,128)(2,1)S(1)}, u32[]{:S(2)}, u32[]{:S(2)}) collective-permute-start(bf16[128,2048]{1,0:T(8,128)(2,1)S(1)} %pad_maximum_fusion.refs_1_), channel_id=1, source_target_pairs={{0,256},{16,272},{32,288},{48,304},{64,320},{80,336},{96,352},{112... | collective-permute-start | bytes 1572872 | tf_op jit(solution)/shard_map/ppermute | solution.py:222
  4.8 0.8 copy-start.1
  6.5 18.4 %all-to-all-start = ((bf16[8,64,256]{2,1,0:T(8,128)(2,1)}), bf16[8,64,256]{2,1,0:T(8,128)(2,1)S(1)}, u32[]{:S(2)}, u32[]{:S(2)}) async-start(bf16[8,64,256]{2,1,0:T(8,128)(2,1)} %shard_map.46), calls=%async_computation | async-start | bytes 524288 | tf_op jit(solution)/shard_map/all_to_all | solution.py:226
  16.5 16.1 %collective-permute-start.1 = (bf16[128,2048]{1,0:T(8,128)(2,1)S(1)}, bf16[128,2048]{1,0:T(8,128)(2,1)S(1)}, u32[]{:S(2)}, u32[]{:S(2)}) collective-permute-start(bf16[128,2048]{1,0:T(8,128)(2,1)S(1)} %pad_maximum_fusion.refs_1_), channel_id=1, source_target_pairs={{0,128},{16,144},{32,160},{48,176},{64,192},{80,208},{96,224},{112... | collective-permute-start | bytes 1572872 | tf_op jit(solution)/shard_map/ppermute | solution.py:222
  19.6 16.9 %collective-permute-start = (bf16[128,2048]{1,0:T(8,128)(2,1)S(1)}, bf16[128,2048]{1,0:T(8,128)(2,1)S(1)}, u32[]{:S(2)}, u32[]{:S(2)}) collective-permute-start(bf16[128,2048]{1,0:T(8,128)(2,1)S(1)} %pad_maximum_fusion.refs_1_), channel_id=1, source_target_pairs={{0,384},{16,400},{32,416},{48,432},{64,448},{80,464},{96,480},{112... | collective-permute-start | bytes 1572872 | tf_op jit(solution)/shard_map/ppermute | solution.py:222
  36.5 45.5 %copy-start = (bf16[1024,1024]{1,0:T(8,128)(2,1)S(1)}, bf16[1024,1024]{1,0:T(8,128)(2,1)}, u32[]{:S(2)}) copy-start(bf16[1024,1024]{1,0:T(8,128)(2,1)} %weight_ref.1) | copy-start | bytes 6291460

commit v7 on v6

--- a/solution.py
+++ b/solution.py
@@ -45,9 +45,10 @@
     )(q)
 
 
-def _attend_kernel(chunks, first, last, *refs):
-    q_ref, kv_refs = refs[0], refs[1 : 1 + chunks]
-    state_ref = None if first else refs[1 + chunks]
+def _attend_kernel(chunks, seen, last, *refs):
+    q_ref, kv_refs, seen_refs = refs[0], refs[1 : 1 + chunks], refs[1 + chunks : 1 + chunks + seen]
+    first = not last and len(refs) == 2 + chunks
+    state_ref = None if first else refs[1 + chunks + seen]
     if last:
         out_ref, hold_ref, pack_ref = refs[-3:]
     else:
@@ -89,17 +90,16 @@
             total = more if total is None else total + more
     hold_ref[0:72, :] = total[0:72]
     hold_ref[72:80, :] = jnp.broadcast_to(peak, (8, rows))
+    if not last:
+        return
     in_range = jnp.max(total[64:65]) < LIMIT
 
     @pl.when(jnp.logical_not(in_range))
     def _():
         q = queries()
-        if first:
-            hold_ref[0:72, :] = jnp.zeros((72, rows), jnp.float32)
-            hold_ref[72:80, :] = jnp.full((8, rows), -1e30, jnp.float32)
-        else:
-            hold_ref[...] = state_ref[...]
-        for kv_ref in kv_refs:
+        hold_ref[0:72, :] = jnp.zeros((72, rows), jnp.float32)
+        hold_ref[72:80, :] = jnp.full((8, rows), -1e30, jnp.float32)
+        for kv_ref in (*seen_refs, *kv_refs):
 
             @pl.loop(0, keys // PART)
             def _(i):
@@ -140,14 +140,14 @@
         out_ref[...] = pack_ref[...].astype(jnp.bfloat16)
 
 
-def _attend(q_all, kvs, state, last):
+def _attend(q_all, kvs, state, seen=(), last=False):
     blocks, _, block = q_all.shape
     rows = blocks * block
     state_type = jax.ShapeDtypeStruct((80, rows), jnp.float32)
-    operands = (q_all, *kvs) + (() if state is None else (state,))
+    operands = (q_all, *kvs, *seen) + (() if state is None else (state,))
     keys = len(kvs) * kvs[0].shape[1]
     return pl.pallas_call(
-        functools.partial(_attend_kernel, len(kvs), state is None, last),
+        functools.partial(_attend_kernel, len(kvs), len(seen), last),
         out_shape=jax.ShapeDtypeStruct((rows // OWN * SENT, WIDE), jnp.bfloat16) if last else state_type,
         in_specs=[pl.BlockSpec(memory_space=pltpu.VMEM)] * len(operands),
         out_specs=pl.BlockSpec(memory_space=pltpu.VMEM),
@@ -225,9 +225,9 @@
     kv2 = swap_x(kv, 2)
     q_all = lax.all_to_all(_copies(queries.T), "views", 0, 0, tiled=True, axis_index_groups=z_groups)
     kv1, kv3 = swap_x(kv, 1), swap_x(kv, 3)
-    state = _attend(q_all, (kv, kv2), None, False)
-    state = _attend(q_all, (kv1,), state, False)
-    rows = _attend(q_all, (kv3,), state, True)
+    state = _attend(q_all, (kv, kv2), None)
+    state = _attend(q_all, (kv1,), state)
+    rows = _attend(q_all, (kv3,), state, (kv, kv2, kv1), True)
 
     sent = rows.reshape(Z * heads * SENT // 2, 2, WIDE)
     got = lax.all_to_all(sent, ("views", "heads"), 0, 0, tiled=True, axis_index_groups=zh_groups)

time: 83.8 us -> 100 us (1.19)
  the two profiles are of different devices: /device:TPU:3 before, /device:TPU:7 now
where the time goes in v7:
time: 100 us; the launch traced here: 99.5 us
  blocking collectives  58.3 us (58%)
  starting transfers between devices  19 us (19%)
  Pallas kernels  17.9 us (18%)
  waiting for transfers between devices  2.38 us (2%)
  other arithmetic  1.06 us (1%)
    all_to_all x1, blocking collectives, per_device(): lax.all_to_all(sent, ('views', 'heads'), 0, 0, tiled=True, axis_index_gro...  58.3 us
    pallas_call x3, Pallas kernels, _attend(): pl.pallas_call(functools.partial(_attend_kernel, len(kvs), len(seen), las...  15.6 us
    all_to_all x1, starting transfers between devices, per_device(): lax.all_to_all(_copies(queries.T), 'views', 0, 0, tiled=True, axis_index_...  10 us
    ppermute x3, starting transfers between devices, swap_x(): return lax.ppermute(array, 'views', pairs)  8.97 us
    all_to_all x1, waiting for transfers between devices, per_device(): lax.all_to_all(_copies(queries.T), 'views', 0, 0, tiled=True, axis_index_...  2.37 us
  transfers between devices with their start and end apart: 4, of which 1 were waited for; matrix products, arithmetic and copies ran while one was open for 0% of the time, Pallas kernels for 12%

profile of v7, /device:TPU:7, one launch (start us, length us, event | category | flops | bytes accessed | tf_op | source)
XLA Modules:
  0.0 99.5 jit_solution(17977908390839224403)
XLA Ops:
  0.0 1.1 %pad_maximum_fusion.refs_1_.refs_2_ = bf16[128,2048]{1,0:T(8,128)(2,1)S(1)} fusion(bf16[64,2048]{1,0:T(8,128)(2,1)} %bitcast.8, bf16[64,2048]{1,0:T(8,128)(2,1)} %bitcast.9), kind=kLoop, calls=%fused_computation | loop fusion | flops 1048576 | bytes 1048576 | tf_op jit(solution)/shard_map/concatenate | solution.py:224
  1.1 3.0 %collective-permute-start.1 = (bf16[128,2048]{1,0:T(8,128)(2,1)S(1)}, bf16[128,2048]{1,0:T(8,128)(2,1)S(1)}, u32[]{:S(2)}, u32[]{:S(2)}) collective-permute-start(bf16[128,2048]{1,0:T(8,128)(2,1)S(1)} %pad_maximum_fusion.refs_1_.refs_2_), channel_id=1, source_target_pairs={{0,256},{16,272},{32,288},{48,304},{64,320},{80,336},{96,352},{112... | collective-permute-start | bytes 1572872 | tf_op jit(solution)/shard_map/ppermute | solution.py:222
  4.1 0.0 copy-start.1
  4.1 0.7 copy-done.1
  4.9 0.9 shard_map.46
  5.8 10.0 %all-to-all-start = ((bf16[8,64,256]{2,1,0:T(8,128)(2,1)}), bf16[8,64,256]{2,1,0:T(8,128)(2,1)S(1)}, u32[]{:S(2)}, u32[]{:S(2)}) async-start(bf16[8,64,256]{2,1,0:T(8,128)(2,1)} %shard_map.46), calls=%async_computation | async-start | bytes 524288 | tf_op jit(solution)/shard_map/all_to_all | solution.py:226
  15.8 1.9 %collective-permute-start.2 = (bf16[128,2048]{1,0:T(8,128)(2,1)S(1)}, bf16[128,2048]{1,0:T(8,128)(2,1)S(1)}, u32[]{:S(2)}, u32[]{:S(2)}) collective-permute-start(bf16[128,2048]{1,0:T(8,128)(2,1)S(1)} %pad_maximum_fusion.refs_1_.refs_2_), channel_id=1, source_target_pairs={{0,128},{16,144},{32,160},{48,176},{64,192},{80,208},{96,224},{112... | collective-permute-start | bytes 1572872 | tf_op jit(solution)/shard_map/ppermute | solution.py:222
  17.7 4.0 %collective-permute-start = (bf16[128,2048]{1,0:T(8,128)(2,1)S(1)}, bf16[128,2048]{1,0:T(8,128)(2,1)S(1)}, u32[]{:S(2)}, u32[]{:S(2)}) collective-permute-start(bf16[128,2048]{1,0:T(8,128)(2,1)S(1)} %pad_maximum_fusion.refs_1_.refs_2_), channel_id=1, source_target_pairs={{0,384},{16,400},{32,416},{48,432},{64,448},{80,464},{96,480},{112... | collective-permute-start | bytes 1572872 | tf_op jit(solution)/shard_map/ppermute | solution.py:222
  21.8 2.4 %all-to-all-done.refs_0_ = bf16[8,64,256]{2,1,0:T(8,128)(2,1)S(1)} async-done(((bf16[8,64,256]{2,1,0:T(8,128)(2,1)}), bf16[8,64,256]{2,1,0:T(8,128)(2,1)S(1)}, u32[]{:S(2)}, u32[]{:S(2)}) %all-to-all-start) | async-done | bytes 262176 | tf_op jit(solution)/shard_map/all_to_all | solution.py:226
  24.1 0.0 collective-permute-done.1.refs_2_.refs_3_
  24.1 7.5 %shard_map.47.refs_2_ = f32[80,2048]{1,0:T(8,128)S(1)} custom-call(bf16[8,64,256]{2,1,0:T(8,128)(2,1)S(1)} %all-to-all-done.refs_0_, bf16[128,2048]{1,0:T(8,128)(2,1)S(1)} %pad_maximum_fusion.refs_1_.refs_2_, bf16[128,2048]{1,0:T(8,128)(2,1)S(1)} %collective-permute-done.1.refs_2_.refs_3_), custom_call_target="tpu_custom_call" | custom-call | flops 8589934592 | bytes 2097152 | tf_op jit(solution)/shard_map/pallas_call | solution.py:149
  31.6 0.0 collective-permute-done.2.refs_1_.refs_4_
  31.6 3.7 %shard_map.48.refs_5_ = f32[80,2048]{1,0:T(8,128)S(1)} custom-call(bf16[8,64,256]{2,1,0:T(8,128)(2,1)S(1)} %all-to-all-done.refs_0_, bf16[128,2048]{1,0:T(8,128)(2,1)S(1)} %collective-permute-done.2.refs_1_.refs_4_, f32[80,2048]{1,0:T(8,128)S(1)} %shard_map.47.refs_2_), custom_call_target="tpu_custom_call" | custom-call | flops 4294967296 | bytes 2097152 | tf_op jit(solution)/shard_map/pallas_call | solution.py:149
  35.4 0.0 collective-permute-done.refs_1_
  35.4 0.0 copy-start
  35.4 4.4 %shard_map.49 = bf16[1280,128]{1,0:T(8,128)(2,1)S(1)} custom-call(bf16[8,64,256]{2,1,0:T(8,128)(2,1)S(1)} %all-to-all-done.refs_0_, bf16[128,2048]{1,0:T(8,128)(2,1)S(1)} %collective-permute-done.refs_1_, bf16[128,2048]{1,0:T(8,128)(2,1)S(1)} %pad_maximum_fusion.refs_1_.refs_2_, bf16[128,2048]{1,0:T(8,128)(2,1)S(1)} %collective-permute-done.1.refs_2_.refs_3_, ...), custom_call_target="tpu_custom_call" | custom-call | flops 4294967296 | bytes 2097152 | tf_op jit(solution)/shard_map/pallas_call | solution.py:149
  39.8 58.3 %all_to_all.10 = bf16[640,2,128]{2,1,0:T(2,128)(2,1)S(1)} all-to-all(bf16[640,2,128]{2,1,0:T(2,128)(2,1)S(1)} %bitcast.6), channel_id=1, replica_groups={{0,1,2,3,4,5,6,7,8,9,10,11,12,13,14,15,32,33,34,35,36,37,38,39,40,41,42..., dimensions={0} | all-to-all | bytes 655360 | tf_op jit(solution)/shard_map/all_to_all | solution.py:233
  98.1 0.0 copy-done
  98.1 1.4 %shard_map.50 = bf16[16,1024]{1,0:T(8,128)(2,1)} custom-call(bf16[1280,128]{1,0:T(8,128)(2,1)S(1)} %bitcast.5, bf16[1024,1024]{1,0:T(8,128)(2,1)S(1)} %copy-done), custom_call_target="tpu_custom_call" | custom-call | tf_op jit(solution)/shard_map/pallas_call | solution.py:206
Async XLA Ops:
  1.1 23.1 %collective-permute-start.1 = (bf16[128,2048]{1,0:T(8,128)(2,1)S(1)}, bf16[128,2048]{1,0:T(8,128)(2,1)S(1)}, u32[]{:S(2)}, u32[]{:S(2)}) collective-permute-start(bf16[128,2048]{1,0:T(8,128)(2,1)S(1)} %pad_maximum_fusion.refs_1_.refs_2_), channel_id=1, source_target_pairs={{0,256},{16,272},{32,288},{48,304},{64,320},{80,336},{96,352},{112... | collective-permute-start | bytes 1572872 | tf_op jit(solution)/shard_map/ppermute | solution.py:222
  4.1 0.8 copy-start.1
  5.8 18.4 %all-to-all-start = ((bf16[8,64,256]{2,1,0:T(8,128)(2,1)}), bf16[8,64,256]{2,1,0:T(8,128)(2,1)S(1)}, u32[]{:S(2)}, u32[]{:S(2)}) async-start(bf16[8,64,256]{2,1,0:T(8,128)(2,1)} %shard_map.46), calls=%async_computation | async-start | bytes 524288 | tf_op jit(solution)/shard_map/all_to_all | solution.py:226
  15.8 15.8 %collective-permute-start.2 = (bf16[128,2048]{1,0:T(8,128)(2,1)S(1)}, bf16[128,2048]{1,0:T(8,128)(2,1)S(1)}, u32[]{:S(2)}, u32[]{:S(2)}) collective-permute-start(bf16[128,2048]{1,0:T(8,128)(2,1)S(1)} %pad_maximum_fusion.refs_1_.refs_2_), channel_id=1, source_target_pairs={{0,128},{16,144},{32,160},{48,176},{64,192},{80,208},{96,224},{112... | collective-permute-start | bytes 1572872 | tf_op jit(solution)/shard_map/ppermute | solution.py:222
  17.7 17.6 %collective-permute-start = (bf16[128,2048]{1,0:T(8,128)(2,1)S(1)}, bf16[128,2048]{1,0:T(8,128)(2,1)S(1)}, u32[]{:S(2)}, u32[]{:S(2)}) collective-permute-start(bf16[128,2048]{1,0:T(8,128)(2,1)S(1)} %pad_maximum_fusion.refs_1_.refs_2_), channel_id=1, source_target_pairs={{0,384},{16,400},{32,416},{48,432},{64,448},{80,464},{96,480},{112... | collective-permute-start | bytes 1572872 | tf_op jit(solution)/shard_map/ppermute | solution.py:222
  35.4 62.7 %copy-start = (bf16[1024,1024]{1,0:T(8,128)(2,1)S(1)}, bf16[1024,1024]{1,0:T(8,128)(2,1)}, u32[]{:S(2)}) copy-start(bf16[1024,1024]{1,0:T(8,128)(2,1)} %weight_ref.1) | copy-start | bytes 6291460
